TPU v7x, 256 devices: a whole 4x4x8 slice. The times are simulated.
256 devices in a mesh: gx: 8 (over x, core), gy: 32 (over z, y).
Axes of the slice: x: 4, y: 4, z: 8, core: 2. Of those that a mesh axis runs over, the one named last changes fastest.
Arguments:
- snapshots: float32 [64, 4, 256, 4096], P(None, None, 'gx', 'gy'), may hold values from -36 to 36
- conductivity: float32 [4, 256, 4096], P(None, 'gx', 'gy'), may hold values from 0.1 to 3
- storage: float32 [4, 256, 4096], P(None, 'gx', 'gy'), may hold values from 0.5 to 2
Outputs:
- basis: float32 [64, 4, 256, 4096], P(None, None, 'gx', 'gy')
- applied: float32 [64, 4, 256, 4096], P(None, None, 'gx', 'gy')
- reduced: float32 [64, 64], replicated
All inputs are finite; a program needn't handle non-finite values.
Results may differ from a plain program's by a relative error of at most 0.00025.
Values sent between devices are 32-bit elements; how exact they have to be, the bound alone decides.
A program may use at most 128 MiB of HBM per device.

v0:
```python
import jax
import jax.numpy as jnp
from jax import lax
from jax.sharding import PartitionSpec as P


def with_halo(cells, sides, width):
    for axis, dim in sides:
        count = lax.axis_size(axis)
        ends = count - 1
        head = lax.slice_in_dim(cells, 0, width, axis=dim)
        tail = lax.slice_in_dim(cells, cells.shape[dim] - width, cells.shape[dim], axis=dim)
        cells = jnp.concatenate(
            [
                lax.ppermute(tail, axis, [(i, (i + 1) % count) for i in range(ends)]),
                cells,
                lax.ppermute(head, axis, [((i + 1) % count, i) for i in range(ends)]),
            ],
            axis=dim,
        )
    return cells


def shifted(padded, step_z, step_x, step_y):
    layer_count = padded.shape[-3] - 2
    row_count = padded.shape[-2] - 2
    column_count = padded.shape[-1] - 2
    return padded[
        ...,
        1 + step_z : 1 + step_z + layer_count,
        1 + step_x : 1 + step_x + row_count,
        1 + step_y : 1 + step_y + column_count,
    ]


def apply_stencil(padded, cond_padded, storage):
    centre = shifted(padded, 0, 0, 0)
    cond_centre = shifted(cond_padded, 0, 0, 0)
    result = storage * centre
    for offset in ((1, 0, 0), (-1, 0, 0), (0, 1, 0), (0, -1, 0), (0, 0, 1), (0, 0, -1)):
        neighbour = shifted(padded, offset[0], offset[1], offset[2])
        cond_near = shifted(cond_padded, offset[0], offset[1], offset[2])
        result = result + 0.5 * (cond_centre + cond_near) * (centre - neighbour)
    return result


def inner(left, right):
    return jnp.dot(
        left, right.T, precision=lax.Precision.HIGHEST, preferred_element_type=jnp.float32
    )


def upper_factor(gram):
    order = gram.shape[0]
    positions = lax.iota(jnp.int32, order)

    def one_column(index, carry):
        remaining, factor = carry
        picker = (positions == index).astype(jnp.float32)
        row_left = jnp.sum(remaining * picker[:, None], axis=0)
        pivot = jnp.sum(row_left * picker)
        row_new = row_left * (positions >= index).astype(jnp.float32) / jnp.sqrt(pivot)
        remaining = remaining - row_new[:, None] * row_new[None, :]
        factor = factor + picker[:, None] * row_new[None, :]
        return (remaining, factor)

    start = (gram, jnp.zeros_like(gram))
    return lax.fori_loop(0, order, one_column, start)[1]


def upper_inverse(factor):
    order = factor.shape[0]
    positions = lax.iota(jnp.int32, order)

    def one_row(turn, inverse):
        index = order - 1 - turn
        picker = (positions == index).astype(jnp.float32)
        factor_row = jnp.sum(factor * picker[:, None], axis=0)
        pivot = jnp.sum(factor_row * picker)
        above = jnp.dot(
            factor_row[None, :],
            inverse,
            precision=lax.Precision.HIGHEST,
            preferred_element_type=jnp.float32,
        )[0]
        row_new = (picker - above) / pivot
        return inverse + picker[:, None] * row_new[None, :]

    return lax.fori_loop(0, order, one_row, jnp.zeros_like(factor))


def solve_upper(inverse, values):
    return jnp.dot(
        inverse.T, values, precision=lax.Precision.HIGHEST, preferred_element_type=jnp.float32
    )


def per_device(snapshots, conductivity, storage):
    basis_size, layer_count, tile_x, tile_y = snapshots.shape
    cell_count = layer_count * tile_x * tile_y * lax.axis_size("gx") * lax.axis_size("gy")
    flat_snap = snapshots.reshape(basis_size, -1)
    cond_rim = with_halo(conductivity, (("gx", 1), ("gy", 2)), 1)
    cond_padded = jnp.pad(cond_rim, ((1, 1), (0, 0), (0, 0)))
    gram_total = lax.psum(inner(flat_snap, flat_snap), ("gx", "gy"))
    inverse = upper_inverse(upper_factor(gram_total / cell_count))
    basis_flat = solve_upper(inverse, flat_snap)
    basis = basis_flat.reshape(snapshots.shape)
    rimmed = with_halo(basis, (("gx", 2), ("gy", 3)), 1)
    padded = jnp.pad(rimmed, ((0, 0), (1, 1), (0, 0), (0, 0)))
    applied = apply_stencil(padded, cond_padded, storage)
    applied_flat = applied.reshape(basis_size, -1)
    reduced = lax.psum(inner(basis_flat, applied_flat), ("gx", "gy")) / cell_count
    return (basis, applied, reduced)


def solution(mesh):
    return jax.shard_map(
        per_device,
        mesh=mesh,
        in_specs=(P(None, None, "gx", "gy"), P(None, "gx", "gy"), P(None, "gx", "gy")),
        out_specs=(P(None, None, "gx", "gy"), P(None, None, "gx", "gy"), P()),
        check_vma=False,
    )
```

profile of v0, /device:TPU:1, one launch (start us, length us, event | category | flops | bytes accessed | tf_op | source)
XLA Modules:
  0.0 470.1 jit_solution(6401949191867084665)
XLA Ops:
  1.4 4.5 collective-permute-start
  5.9 1.9 collective-permute-start.1
  7.8 11.4 %fusion.39 = f32[64,64]{1,0:T(8,128)S(1)} fusion(f32[64,4,32,128]{3,2,1,0:T(8,128)} %param.7), kind=kOutput, calls=%fused_computation.64 | convolution fusion | flops 805306368 | bytes 4210688 | tf_op jit(solution)/shard_map/dot_general | solution.py:48
  19.2 79.8 %psum.14 = f32[64,64]{1,0:T(8,128)S(1)} all-reduce(f32[64,64]{1,0:T(8,128)S(1)} %fusion.39), channel_id=1, replica_groups=mesh['gx'=8,'gy'=32] {'gx','gy'}, use_global_device_ids=true, to_apply=%region_0.1 | all-reduce | flops 4096 | bytes 32768 | tf_op jit(solution)/shard_map/psum | solution.py:104
  99.1 97.7 %while.32 = (s32[]{:T(128)}, f32[64,64]{1,0:T(8,128)S(1)}, f32[64,64]{1,0:T(8,128)S(1)}, s32[]{:T(128)}, s32[]{:T(128)}) while((s32[]{:T(128)}, f32[64,64]{1,0:T(8,128)S(1)}, f32[64,64]{1,0:T(8,128)S(1)}, s32[]{:T(128)}, s32[]{:T(128)}) %tuple.84), condition=%wide.region_4.5_spmd.clone.clone, body=%wide.region_1.4_spmd.clone.clone.sunk | while | flops 29122 | bytes 84075 | solution.py:68
  196.8 101.2 %while.31 = (s32[]{:T(128)}, f32[64,64]{1,0:T(8,128)S(1)}, f32[64,64]{1,0:T(8,128)S(1)}, s32[]{:T(128)}, s32[]{:T(128)}, /*index=5*/s32[]{:T(128)}) while((s32[]{:T(128)}, f32[64,64]{1,0:T(8,128)S(1)}, f32[64,64]{1,0:T(8,128)S(1)}, s32[]{:T(128)}, s32[]{:T(128)}, /*index=5*/s32[]{:T(128)}) %tuple.87), condition=%wide.region_8.9_spmd.clone, body=%wide.region_5.8_spmd.clone.sunk | while | flops 74243 | bytes 67704 | solution.py:89
  197.5 0.8 fusion.67
  199.1 0.8 fusion.67
  200.6 0.8 fusion.67
  202.2 0.8 fusion.67
  203.8 0.8 fusion.67
  205.4 0.8 fusion.67
  207.0 0.8 fusion.67
  208.6 0.8 fusion.67
  210.1 0.8 fusion.67
  211.7 0.8 fusion.67
  213.3 0.8 fusion.67
  216.5 0.8 fusion.67
  218.0 0.8 fusion.67
  221.2 0.8 fusion.67
  222.8 0.8 fusion.67
  225.9 0.8 fusion.67
  229.1 0.8 fusion.67
  230.7 0.8 fusion.67
  233.8 0.8 fusion.67
  235.4 0.8 fusion.67
  238.6 0.8 fusion.67
  243.3 0.8 fusion.67
  246.5 0.8 fusion.67
  248.1 0.8 fusion.67
  251.2 0.8 fusion.67
  252.8 0.8 fusion.67
  256.0 0.8 fusion.67
  259.1 0.8 fusion.67
  260.7 0.8 fusion.67
  263.9 0.8 fusion.67
  265.5 0.8 fusion.67
  268.6 0.8 fusion.67
  273.4 0.8 fusion.67
  276.5 0.8 fusion.67
  278.1 0.8 fusion.67
  281.3 0.8 fusion.67
  282.9 0.8 fusion.67
  286.0 0.8 fusion.67
  289.2 0.8 fusion.67
  290.8 0.8 fusion.67
  293.9 0.8 fusion.67
  295.5 0.8 fusion.67
  298.0 8.4 %fusion.34 = f32[64,16384]{1,0:T(8,128)S(1)} fusion(f32[64,64]{1,0:T(8,128)S(1)} %get-tuple-element.165, f32[8,8,128,128]{3,2,1,0:T(8,128)} %bitcast.37), kind=kOutput, calls=%fused_computation.59 | convolution fusion | flops 805306368 | bytes 8404992 | tf_op jit(solution)/shard_map/dot_general | solution.py:93
  306.4 1.9 copy-done
  309.1 2.0 copy-done.1
  311.3 2.6 collective-permute-start.5
  313.9 3.0 collective-permute-start.4
  317.0 1.3 collective-permute-start.3
  318.3 4.0 collective-permute-start.2
  322.3 9.2 %copy.109 = f32[64,4,32,128]{0,2,3,1:T(8,128)} copy(f32[64,4,32,128]{3,2,1,0:T(8,128)} %bitcast.34) | data formatting | bytes 8388608 | tf_op jit(solution)/shard_map/reshape | solution.py:107
  332.1 0.9 pad_maximum_fusion.8
  333.1 1.3 collective-permute-start.7
  334.4 4.2 collective-permute-start.6
  339.8 7.1 %select_maximum_fusion = f32[64,6,34,130]{0,2,3,1:T(8,128)S(1)} fusion(f32[64,4,34,1]{0,2,3,1:T(8,128)S(1)} %collective-permute-done.7, f32[64,4,34,1]{0,2,3,1:T(8,128)S(1)} %collective-permute-done.6, f32[64,4,1,128]{0,2,3,1:T(1,128)S(1)} %copy.115, f32[64,4,32,128]{0,2,3,1:T(8,128)} %copy.109, f32[64,4,1,128]{0,2,3,1:T(1,128)S(1)} %copy.113), kind=kLoop, calls=%fused_computation.25 | loop fusion | flops 20367360 | bytes 11315200 | tf_op jit(solution)/shard_map/concatenate | solution.py:13
  347.0 23.8 %fusion.17 = f32[64,4,32,128]{0,2,3,1:T(8,128)} fusion(f32[64,4,32,128]{0,2,3,1:T(8,128)} %copy.109, f32[64,4,34,1]{0,2,3,1:T(8,128)S(1)} %collective-permute-done.6, f32[64,4,1,128]{0,2,3,1:T(1,128)S(1)} %copy.115, f32[64,4,1,128]{0,2,3,1:T(1,128)S(1)} %copy.113, f32[64,4,34,1]{0,2,3,1:T(8,128)S(1)} %collective-permute-done.7, ...), kind=kLoop, calls=%fused_computation.33 | loop fusion | flops 28311552 | bytes 17567744 | tf_op jit(solution)/shard_map/add | solution.py:43
  370.7 8.7 %copy.132 = f32[64,4,32,128]{3,2,1,0:T(8,128)} copy(f32[64,4,32,128]{0,2,3,1:T(8,128)} %fusion.17) | data formatting | bytes 8388608
  379.4 9.0 %fusion.31 = f32[64,64]{1,0:T(8,128)S(1)} fusion(f32[64,16384]{1,0:T(8,128)} %copy-done, f32[8,8,128,128]{3,2,1,0:T(8,128)} %bitcast.36), kind=kOutput, calls=%fused_computation.56 | convolution fusion | flops 805306368 | bytes 8404992 | tf_op jit(solution)/shard_map/dot_general | solution.py:48
  388.5 81.0 %psum.15 = f32[64,64]{1,0:T(8,128)S(1)} all-reduce(f32[64,64]{1,0:T(8,128)S(1)} %fusion.31), channel_id=1, replica_groups=mesh['gx'=8,'gy'=32] {'gx','gy'}, use_global_device_ids=true, to_apply=%region_9.10 | all-reduce | flops 4096 | bytes 32768 | tf_op jit(solution)/shard_map/psum | solution.py:112
  (634 shorter events, 122.6 us)
Async XLA Ops:
  1.4 315.5 %collective-permute-start = (f32[4,1,128]{2,1,0:T(1,128)S(1)}, f32[4,1,128]{2,1,0:T(1,128)S(1)}, u32[]{:S(2)}, u32[]{:S(2)}) collective-permute-start(f32[4,1,128]{2,1,0:T(1,128)S(1)} %get-tuple-element.249), channel_id=1, source_target_pairs={{0,32},{32,64},{64,96},{96,128},{128,160},{160,192},{192,224},{1,3... | collective-permute-start | bytes 6152 | tf_op jit(solution)/shard_map/ppermute | solution.py:15
  5.9 311.0 %collective-permute-start.1 = (f32[4,1,128]{2,1,0:T(1,128)S(1)}, f32[4,1,128]{2,1,0:T(1,128)S(1)}, u32[]{:S(2)}, u32[]{:S(2)}) collective-permute-start(f32[4,1,128]{2,1,0:T(1,128)S(1)} %get-tuple-element.250), channel_id=1, source_target_pairs={{32,0},{64,32},{96,64},{128,96},{160,128},{192,160},{224,192},{33,... | collective-permute-start | bytes 6152 | tf_op jit(solution)/shard_map/ppermute | solution.py:17
  298.0 19.0 %copy-start.2 = (f32[4,32,128]{2,1,0:T(8,128)S(1)}, f32[4,32,128]{2,1,0:T(8,128)}, u32[]{:S(2)}) copy-start(f32[4,32,128]{2,1,0:T(8,128)} %param.8) | copy-start | bytes 196612
  306.4 1.9 copy-start
  309.1 2.0 copy-start.1
  309.1 22.4 %copy-start.3 = (f32[4,32,128]{2,1,0:T(8,128)S(1)}, f32[4,32,128]{2,1,0:T(8,128)}, u32[]{:S(2)}) copy-start(f32[4,32,128]{2,1,0:T(8,128)} %param.9) | copy-start | bytes 196612
  311.3 20.6 %collective-permute-start.5 = (f32[64,4,1,128]{3,0,2,1:T(8,128)S(1)}, f32[64,4,1,128]{3,0,2,1:T(8,128)S(1)}, u32[]{:S(2)}, u32[]{:S(2)}) collective-permute-start(f32[64,4,1,128]{3,0,2,1:T(8,128)S(1)} %copy.135), channel_id=1, source_target_pairs={{32,0},{64,32},{96,64},{128,96},{160,128},{192,160},{224,192},{33,... | collective-permute-start | bytes 393224 | tf_op jit(solution)/shard_map/ppermute | solution.py:17
  313.9 18.1 %collective-permute-start.4 = (f32[64,4,1,128]{3,0,2,1:T(8,128)S(1)}, f32[64,4,1,128]{3,0,2,1:T(8,128)S(1)}, u32[]{:S(2)}, u32[]{:S(2)}) collective-permute-start(f32[64,4,1,128]{3,0,2,1:T(8,128)S(1)} %copy.134), channel_id=1, source_target_pairs={{0,32},{32,64},{64,96},{96,128},{128,160},{160,192},{192,224},{1,3... | collective-permute-start | bytes 393224 | tf_op jit(solution)/shard_map/ppermute | solution.py:15
  317.0 14.6 %collective-permute-start.3 = (f32[4,34,1]{2,1,0:T(8,128)S(1)}, f32[4,34,1]{2,1,0:T(8,128)S(1)}, u32[]{:S(2)}, u32[]{:S(2)}) collective-permute-start(f32[4,34,1]{2,1,0:T(8,128)S(1)} %get-tuple-element.241), channel_id=1, source_target_pairs={{1,0},{2,1},{3,2},{4,3},{5,4},{6,5},{7,6},{8,7},{9,8},{10,9},{11,1... | collective-permute-start | bytes 1640 | tf_op jit(solution)/shard_map/ppermute | solution.py:17
  318.3 13.4 %collective-permute-start.2 = (f32[4,34,1]{2,1,0:T(8,128)S(1)}, f32[4,34,1]{2,1,0:T(8,128)S(1)}, u32[]{:S(2)}, u32[]{:S(2)}) collective-permute-start(f32[4,34,1]{2,1,0:T(8,128)S(1)} %get-tuple-element.242), channel_id=1, source_target_pairs={{0,1},{1,2},{2,3},{3,4},{4,5},{5,6},{6,7},{7,8},{8,9},{9,10},{10,1... | collective-permute-start | bytes 1640 | tf_op jit(solution)/shard_map/ppermute | solution.py:15
  333.1 6.5 %collective-permute-start.7 = (f32[64,4,34,1]{0,2,3,1:T(8,128)S(1)}, f32[64,4,34,1]{0,2,3,1:T(8,128)S(1)}, u32[]{:S(2)}, u32[]{:S(2)}) collective-permute-start(f32[64,4,34,1]{0,2,3,1:T(8,128)S(1)} %get-tuple-element.235), channel_id=1, source_target_pairs={{1,0},{2,1},{3,2},{4,3},{5,4},{6,5},{7,6},{8,7},{9,8},{10,9},{11,1... | collective-permute-start | bytes 104456 | tf_op jit(solution)/shard_map/ppermute | solution.py:17
  334.4 5.5 %collective-permute-start.6 = (f32[64,4,34,1]{0,2,3,1:T(8,128)S(1)}, f32[64,4,34,1]{0,2,3,1:T(8,128)S(1)}, u32[]{:S(2)}, u32[]{:S(2)}) collective-permute-start(f32[64,4,34,1]{0,2,3,1:T(8,128)S(1)} %get-tuple-element.236), channel_id=1, source_target_pairs={{0,1},{1,2},{2,3},{3,4},{4,5},{5,6},{6,7},{7,8},{8,9},{9,10},{10,1... | collective-permute-start | bytes 104456 | tf_op jit(solution)/shard_map/ppermute | solution.py:15
where the time goes:
time: 473 us; the launch traced here: 470 us
  blocking collectives  161 us (34%)
  other arithmetic  134 us (28%)
  matrix products  79 us (17%)
  loops' own time  47.6 us (10%)
  local copies, waits for them, and re-layouts  24.8 us (5%)
  starting transfers between devices  22.8 us (5%)
    psum x1, blocking collectives, per_device(): lax.psum(inner(basis_flat, applied_flat), ('gx', 'gy')) / cell_count  81 us
    psum x1, blocking collectives, per_device(): gram_total = lax.psum(inner(flat_snap, flat_snap), ('gx', 'gy'))  79.8 us
    dot_general x64, matrix products, one_row(): jnp.dot(factor_row[None, :], inverse, precision=lax.Precision.HIGHEST, pr...  50.1 us
    another operation x1, loops' own time, upper_factor(): return lax.fori_loop(0, order, one_column, start)[1]  46.9 us
    reduce_sum x64, other arithmetic, one_row(): pivot = jnp.sum(factor_row * picker)  38.7 us
    reduce_sum x64, other arithmetic, one_column(): pivot = jnp.sum(row_left * picker)  38.7 us
    add x1, other arithmetic, apply_stencil(): result = result + 0.5 * (cond_centre + cond_near) * (centre - neighbour)  23.8 us
    dot_general x2, matrix products, inner(): jnp.dot(left, right.T, precision=lax.Precision.HIGHEST, preferred_element...  20.4 us
  transfers between devices with their start and end apart: 8, of which 1 were waited for; matrix products, arithmetic and copies ran while one was open for 39% of the time, Pallas kernels for 0%

commit v1 on v0

v1 whole, which is shorter than its diff:
```python
import functools

import jax
import jax.numpy as jnp
from jax import lax
from jax.experimental import pallas as pl
from jax.experimental.pallas import tpu as pltpu
from jax.sharding import PartitionSpec as P

MESH = pl.DeviceIdType.MESH
F32 = jnp.float32
BF16 = jnp.bfloat16
K = 64
LAYERS = 4
TX = 32
TY = 128
CELLS = LAYERS * TX
XY = 16
Z = 8
COUNT = 4 * 256 * 4096


def split(value):
    high = value.astype(BF16)
    low = (value - high.astype(F32)).astype(BF16)
    return high, low


def product_nt(left, right):
    return lax.dot_general(left, right, (((1,), (1,)), ((), ())), preferred_element_type=F32)


def lanes(shape):
    return lax.broadcasted_iota(jnp.int32, shape, len(shape) - 1)


def rows(shape):
    return lax.broadcasted_iota(jnp.int32, shape, len(shape) - 2)


def folded(matrix):
    return [
        jnp.concatenate([matrix[32 * h : 32 * h + 16], matrix[32 * h + 16 : 32 * h + 32]], axis=1)
        for h in range(2)
    ]


def unfolded(halves):
    return jnp.concatenate(
        [part for h in halves for part in (h[:, :64], h[:, 64:])], axis=0
    )


class Total:
    def __init__(self, place, packed, pair, plane, column, whole, send, recv):
        self.x, self.y, self.z, self.core = place
        self.packed, self.pair, self.plane, self.column, self.whole = packed, pair, plane, column, whole
        self.send, self.recv = send, recv

    def device(self, x, y, z, core):
        return (x * 2 + core, z * 4 + y)

    def copy(self, src, dst, step, device):
        pltpu.make_async_remote_copy(
            src_ref=src,
            dst_ref=dst,
            send_sem=self.send.at[step],
            recv_sem=self.recv.at[step],
            device_id=device,
            device_id_type=MESH,
        ).start()

    def other_core(self):
        return self.device(self.x, self.y, self.z, 1 - self.core)

    def plane_peers(self):
        return [
            self.device(lax.rem(self.x + i, 4), lax.rem(self.y + j, 4), self.z, self.core)
            for i in range(4)
            for j in range(4)
            if i or j
        ]

    def column_peers(self):
        return [self.device(self.x, self.y, lax.rem(self.z + i, Z), self.core) for i in range(1, Z)]

    def start_pair(self, matrix):
        for h, half in enumerate(folded(matrix)):
            self.packed[h] = half
        self.copy(self.packed.at[1 - self.core], self.pair, 0, self.other_core())

    def start_plane(self):
        pltpu.make_async_copy(self.pair, self.pair, self.recv.at[0]).wait()
        me = self.x * 4 + self.y
        self.plane[me] = self.packed[self.core] + self.pair[...]
        for peer in self.plane_peers():
            self.copy(self.plane.at[me], self.plane.at[me], 1, peer)

    def start_column(self):
        rest = self.plane.at[pl.ds(0, XY - 1)]
        pltpu.make_async_copy(rest, rest, self.recv.at[1]).wait()
        total = self.plane[0]
        for i in range(1, XY):
            total = total + self.plane[i]
        self.column[self.z] = total
        for peer in self.column_peers():
            self.copy(self.column.at[self.z], self.column.at[self.z], 2, peer)

    def start_whole(self):
        rest = self.column.at[pl.ds(0, Z - 1)]
        pltpu.make_async_copy(rest, rest, self.recv.at[2]).wait()
        total = self.column[0]
        for i in range(1, Z):
            total = total + self.column[i]
        self.whole[self.core] = total
        self.copy(self.whole.at[self.core], self.whole.at[self.core], 3, self.other_core())

    def result(self):
        pltpu.make_async_copy(self.whole.at[0], self.whole.at[0], self.recv.at[3]).wait()
        return unfolded([self.whole[0], self.whole[1]])

    def drain(self):
        for step, ref in enumerate(
            (
                self.pair,
                self.plane.at[pl.ds(0, XY - 1)],
                self.column.at[pl.ds(0, Z - 1)],
                self.whole.at[0],
            )
        ):
            pltpu.make_async_copy(ref, ref, self.send.at[step]).wait()


def eliminated(matrix):
    eye = (rows((K, K)) == lanes((K, K))).astype(F32)
    whole = jnp.concatenate([matrix, eye], axis=1)
    blocks = [whole[8 * i : 8 * i + 8] for i in range(8)]
    sub = rows((8, 2 * K))
    for b in range(8):
        columns = [
            {i: jnp.broadcast_to(blocks[i][:, 8 * b + c : 8 * b + c + 1], (8, 2 * K)) for i in range(b, 8)}
            for c in range(8)
        ]
        for c in range(8):
            pivot = jnp.broadcast_to(columns[c][b][c : c + 1], (8, 2 * K))
            inverse = 1.0 / pivot
            pivot_row = jnp.broadcast_to(blocks[b][c : c + 1], (8, 2 * K))
            later = [jnp.broadcast_to(columns[d][b][c : c + 1], (8, 2 * K)) for d in range(c + 1, 8)]
            for i in range(b, 8):
                factor = columns[c][i] * inverse
                if i == b:
                    factor = jnp.where(sub > c, factor, 0.0)
                for at, d in enumerate(range(c + 1, 8)):
                    columns[d][i] = columns[d][i] - factor * later[at]
                blocks[i] = blocks[i] - factor * pivot_row
    whole = jnp.concatenate(blocks, axis=0)
    diagonal = rows((K, 2 * K)) == lanes((K, 2 * K))
    pivots = jnp.sum(jnp.where(diagonal, whole, 0.0), axis=1, keepdims=True)
    return whole[:, K:] * (1.0 / jnp.sqrt(pivots))


def gather_kernel(
    snap_any, cond_any, stor_any,
    snap_out, flux_out, weights_out, reduced_out,
    natural, field, cond, stor, padded, coefs, edges, flat,
    gram_acc, proj_acc,
    side_send, side_cond_send, side_cond, end_send, end_got,
    g_packed, g_pair, g_plane, g_column, g_whole,
    m_packed, m_pair, m_plane, m_column, m_whole,
    load_sem, halo_send, halo_recv, g_send, g_recv, m_send, m_recv,
):
    gx, gy = lax.axis_index("gx"), lax.axis_index("gy")
    place = (gx // 2, lax.rem(gy, 4), gy // 4, lax.rem(gx, 2))
    gram_total = Total(place, g_packed, g_pair, g_plane, g_column, g_whole, g_send, g_recv)
    proj_total = Total(place, m_packed, m_pair, m_plane, m_column, m_whole, m_send, m_recv)

    natural3 = natural.reshape(K, CELLS, TY)
    loads = []
    for l in range(LAYERS):
        part = pl.ds(l * TX, TX)
        loads.append(pltpu.make_async_copy(snap_any.at[:, part], natural3.at[:, part], load_sem.at[l]))
    loads.append(pltpu.make_async_copy(cond_any, cond, load_sem.at[LAYERS]))
    loads.append(pltpu.make_async_copy(stor_any, stor, load_sem.at[LAYERS + 1]))
    for load in loads:
        load.start()

    x_left = (lax.rem(gx + 7, 8), gy)
    x_right = (lax.rem(gx + 1, 8), gy)
    y_left = (gx, lax.rem(gy + 31, 32))
    y_right = (gx, lax.rem(gy + 1, 32))
    barrier = pltpu.get_barrier_semaphore()
    partners = [gram_total.other_core(), *gram_total.plane_peers(), *gram_total.column_peers()]
    partners += [x_left, x_right, y_left, y_right]
    for partner in partners:
        pl.semaphore_signal(barrier, inc=1, device_id=partner, device_id_type=MESH)

    gram_acc[...] = jnp.zeros_like(gram_acc)
    proj_acc[...] = jnp.zeros_like(proj_acc)
    lane = lanes((K, TY))

    for l in range(LAYERS):
        loads[l].wait()

        def four_rows(turn, carry):
            highs, lows = [], []
            for d in range(4):
                x = turn * 4 + d
                cell = l * TX + x
                value = natural[pl.ds(cell, K, stride=CELLS), :]
                field[x + 1, l] = value
                high, low = split(value)
                snap_out[cell, 0:K] = high
                snap_out[cell, K : 2 * K] = low
                turned = pltpu.roll(value, cell, 1)
                here = (lane == cell) | (lane == lax.rem(cell + TY - 1, TY))
                edges[d % 2] = jnp.where(here, turned, edges[d % 2])
                highs.append(high)
                lows.append(low)
            high = jnp.concatenate(highs, axis=1)
            low = jnp.concatenate(lows, axis=1)
            gram_acc[...] += product_nt(jnp.concatenate([high, low], axis=0), high)
            return carry

        lax.fori_loop(0, TX // 4, four_rows, 0)

    loads[LAYERS].wait()
    loads[LAYERS + 1].wait()

    even = lax.rem(lane, 2) == 0
    end_send[0, 0:K] = jnp.where(even, edges[0], edges[1])
    end_send[1, 0:K] = jnp.where(even, edges[1], edges[0])
    lane8 = lanes((8, TY))
    ends = jnp.zeros((8, TY), F32)
    for i in range(16):
        value = cond[8 * i : 8 * i + 8, :]
        ends = jnp.where(lane8 == i, pltpu.roll(value, i, 1) if i else value, ends)
        ends = jnp.where(lane8 == 16 + i, pltpu.roll(value, 17 + i, 1), ends)
    end_send[0, K : K + 8] = ends
    end_send[1, K : K + 8] = ends
    side_cond_send[...] = jnp.zeros_like(side_cond_send)
    for l in range(LAYERS):
        side_cond_send[0, l : l + 1] = cond[l * TX : l * TX + 1, :]
        side_cond_send[1, l : l + 1] = cond[l * TX + TX - 1 : l * TX + TX, :]

    cross = gram_acc[K : 2 * K]
    gram_part = gram_acc[0:K] + (cross + cross.T)

    pl.semaphore_wait(barrier, len(partners))
    gram_total.start_pair(gram_part)

    def halo(src, dst, which, device):
        copy = pltpu.make_async_remote_copy(
            src_ref=src, dst_ref=dst, send_sem=halo_send.at[which], recv_sem=halo_recv.at[which],
            device_id=device, device_id_type=MESH,
        )
        copy.start()
        return copy

    halos = [
        halo(side_cond_send.at[0], side_cond.at[1], 0, x_left),
        halo(side_cond_send.at[1], side_cond.at[0], 1, x_right),
        halo(end_send.at[0], end_got.at[1], 2, y_left),
        halo(end_send.at[1], end_got.at[0], 3, y_right),
        halo(field.at[1], field.at[TX + 1], 4, x_left),
        halo(field.at[TX], field.at[0], 5, x_right),
    ]
    gram_total.start_plane()

    for copy in halos:
        copy.wait_recv()

    first_x, last_x = gx == 0, gx == 7
    first_y, last_y = gy == 0, gy == 31
    for l in range(LAYERS):
        padded[l, 8 : 8 + TX] = cond[l * TX : l * TX + TX, :]
        padded[l, 7:8] = jnp.where(first_x, 0.0, side_cond[0, l : l + 1])
        padded[l, 8 + TX : 9 + TX] = jnp.where(last_x, 0.0, side_cond[1, l : l + 1])
    row8 = rows((8, TY))
    for l in range(LAYERS):
        for b in range(TX // 8):
            at = l * TX + 8 * b
            i = at // 8
            here = padded[l, 8 + 8 * b : 16 + 8 * b]
            x_up = 0.5 * (here + padded[l, 9 + 8 * b : 17 + 8 * b])
            x_down = 0.5 * (here + padded[l, 7 + 8 * b : 15 + 8 * b])
            l_up = 0.5 * (here + padded[l + 1, 8 + 8 * b : 16 + 8 * b]) if l + 1 < LAYERS else 0.5 * here
            l_down = 0.5 * (here + padded[l - 1, 8 + 8 * b : 16 + 8 * b]) if l else 0.5 * here
            left = jnp.where(first_y, 0.0, pltpu.roll(end_got[0, K : K + 8], TY - 16 - i, 1))
            right = jnp.where(last_y, 0.0, pltpu.roll(end_got[1, K : K + 8], TY - 1 - i, 1))
            y_down = 0.5 * (here + jnp.where(lane8 == 0, left, pltpu.roll(here, 1, 1)))
            y_up = 0.5 * (here + jnp.where(lane8 == TY - 1, right, pltpu.roll(here, TY - 1, 1)))
            centre = stor[at : at + 8, :] + x_up + x_down + l_up + l_down + y_up + y_down
            span = slice(at, at + 8)
            coefs[0, span] = centre
            coefs[1, span] = jnp.where(last_x & (row8 == 7), 0.0, x_up) if b == TX // 8 - 1 else x_up
            coefs[2, span] = jnp.where(first_x & (row8 == 0), 0.0, x_down) if b == 0 else x_down
            coefs[3, span] = l_up
            coefs[4, span] = l_down
            coefs[5, span] = jnp.where(lane8 == TY - 1, 0.0, y_up)
            coefs[6, span] = jnp.where(lane8 == 0, 0.0, y_down)
            coefs[7, span] = jnp.where(
                lane8 == 0,
                jnp.where(first_y, 0.0, y_down),
                jnp.where(lane8 == TY - 1, jnp.where(last_y, 0.0, y_up), 0.0),
            )

    from_left = pltpu.roll(end_got[0, 0:K], 1, 1)
    from_right = pltpu.roll(end_got[1, 0:K], TY - 1, 1)
    flat[0] = jnp.where(even, from_left, from_right)
    flat[1] = jnp.where(even, from_right, from_left)

    def two_rows(turn, carry):
        for d in range(2):
            x = turn * 2 + d
            for l in range(LAYERS):
                cell = l * TX + x
                coef = [coefs[i, pl.ds(cell, 1), :] for i in range(8)]
                here = field[x + 1, l]
                value = coef[0] * here
                value = value - coef[1] * field[x + 2, l]
                value = value - coef[2] * field[x, l]
                if l + 1 < LAYERS:
                    value = value - coef[3] * field[x + 1, l + 1]
                if l:
                    value = value - coef[4] * field[x + 1, l - 1]
                value = value - coef[5] * pltpu.roll(here, TY - 1, 1)
                value = value - coef[6] * pltpu.roll(here, 1, 1)
                value = value - coef[7] * pltpu.roll(flat[d], lax.rem(TY - cell, TY), 1)
                high, low = split(value)
                flux_out[cell, 0:K] = high
                flux_out[cell, K : 2 * K] = low
        cells = [l * TX + turn * 2 + d for d in range(2) for l in range(LAYERS)]
        proj_acc[...] += product_nt(
            jnp.concatenate([snap_out[cell] for cell in cells], axis=1),
            jnp.concatenate([flux_out[cell] for cell in cells], axis=1),
        )
        return carry

    lax.fori_loop(0, TX // 4, two_rows, 0)
    gram_total.start_column()
    lax.fori_loop(TX // 4, TX // 2, two_rows, 0)
    proj_part = (
        proj_acc[0:K, 0:K] + (proj_acc[K : 2 * K, 0:K] + proj_acc[0:K, K : 2 * K]) + proj_acc[K : 2 * K, K : 2 * K]
    )
    proj_total.start_pair(proj_part)
    proj_total.start_plane()
    gram_total.start_whole()
    weights = eliminated(gram_total.result() * (1.0 / COUNT))
    high, low = split(weights)
    weights_out[...] = jnp.concatenate([high, high, low, low], axis=1)
    proj_total.start_column()
    proj_total.start_whole()
    exact = dict(precision=lax.Precision.HIGHEST, preferred_element_type=F32)
    half = jnp.dot(weights, proj_total.result(), **exact)
    reduced_out[...] = lax.dot_general(half, weights, (((1,), (1,)), ((), ())), **exact) * (1.0 / COUNT)
    for copy in halos:
        copy.wait_send()
    gram_total.drain()
    proj_total.drain()


def gathered(snapshots, conductivity, storage):
    any_spec = pl.BlockSpec(memory_space=pltpu.HBM)
    vmem_spec = pl.BlockSpec(memory_space=pltpu.VMEM)
    total = [
        pltpu.VMEM((2, 16, 128), F32),
        pltpu.VMEM((16, 128), F32),
        pltpu.VMEM((XY, 16, 128), F32),
        pltpu.VMEM((Z, 16, 128), F32),
        pltpu.VMEM((2, 16, 128), F32),
    ]
    dma = pltpu.SemaphoreType.DMA
    return pl.pallas_call(
        gather_kernel,
        out_shape=(
            pltpu.VMEM((CELLS, 2 * K, TY), BF16),
            pltpu.VMEM((CELLS, 2 * K, TY), BF16),
            pltpu.VMEM((K, 4 * K), BF16),
            pltpu.VMEM((K, K), F32),
        ),
        in_specs=[any_spec] * 3,
        out_specs=(vmem_spec,) * 4,
        scratch_shapes=[
            pltpu.VMEM((K * CELLS, TY), F32),
            pltpu.VMEM((TX + 2, LAYERS, K, TY), F32),
            pltpu.VMEM((CELLS, TY), F32),
            pltpu.VMEM((CELLS, TY), F32),
            pltpu.VMEM((LAYERS, TX + 16, TY), F32),
            pltpu.VMEM((8, CELLS, TY), F32),
            pltpu.VMEM((2, K, TY), F32),
            pltpu.VMEM((2, K, TY), F32),
            pltpu.VMEM((2 * K, K), F32),
            pltpu.VMEM((2 * K, 2 * K), F32),
            pltpu.VMEM((LAYERS // 2, 8, TY), F32),
            pltpu.VMEM((2, 8, TY), F32),
            pltpu.VMEM((2, 8, TY), F32),
            pltpu.VMEM((2, K + 8, TY), F32),
            pltpu.VMEM((2, K + 8, TY), F32),
            *total,
            *total,
            dma((LAYERS + 2,)),
            dma((6,)),
            dma((6,)),
            dma((4,)),
            dma((4,)),
            dma((4,)),
            dma((4,)),
        ],
        compiler_params=pltpu.CompilerParams(
            collective_id=0, has_side_effects=True, vmem_limit_bytes=40 * 2**20
        ),
    )(
        snapshots.reshape(K, CELLS, TY),
        conductivity.reshape(CELLS, TY),
        storage.reshape(CELLS, TY),
    )


PART = 16


def expand_kernel(snap, flux, weights, reduced_in, basis, applied, reduced, basis_held, applied_held, sems):
    reduced[...] = reduced_in[...]
    copies = []
    for part in range(CELLS // PART):

        def two_cells(turn, carry):
            cell = part * PART + turn * 2
            for source, held in ((snap, basis_held), (flux, applied_held)):
                pair = jnp.concatenate([source[cell], source[cell + 1]], axis=1)
                out = jnp.dot(
                    weights[...], jnp.concatenate([pair, pair], axis=0), preferred_element_type=F32
                )
                held[pl.ds(cell, K, stride=CELLS), :] = out[:, :TY]
                held[pl.ds(cell + 1, K, stride=CELLS), :] = out[:, TY:]
            return carry

        lax.fori_loop(0, PART // 2, two_cells, 0)
        span = pl.ds(part * PART, PART)
        for which, (held, target) in enumerate(((basis_held, basis), (applied_held, applied))):
            copy = pltpu.make_async_copy(
                held.reshape(K, CELLS, TY).at[:, span], target.at[:, span], sems.at[which, part]
            )
            copy.start()
            copies.append(copy)
    for copy in copies:
        copy.wait()


def expanded(snap, flux, weights, reduced):
    vmem_spec = pl.BlockSpec(memory_space=pltpu.VMEM)
    any_spec = pl.BlockSpec(memory_space=pltpu.HBM)
    shape = jax.ShapeDtypeStruct((K, CELLS, TY), F32)
    return pl.pallas_call(
        expand_kernel,
        out_shape=(shape, shape, jax.ShapeDtypeStruct((K, K), F32)),
        in_specs=[vmem_spec] * 4,
        out_specs=(any_spec, any_spec, vmem_spec),
        scratch_shapes=[
            pltpu.VMEM((K * CELLS, TY), F32),
            pltpu.VMEM((K * CELLS, TY), F32),
            pltpu.SemaphoreType.DMA((2, CELLS // PART)),
        ],
        compiler_params=pltpu.CompilerParams(vmem_limit_bytes=40 * 2**20),
    )(snap, flux, weights, reduced)


def per_device(snapshots, conductivity, storage):
    basis, applied, reduced = expanded(*gathered(snapshots, conductivity, storage))
    return (basis.reshape(snapshots.shape), applied.reshape(snapshots.shape), reduced)


def solution(mesh):
    return jax.shard_map(
        per_device,
        mesh=mesh,
        in_specs=(P(None, None, "gx", "gy"), P(None, "gx", "gy"), P(None, "gx", "gy")),
        out_specs=(P(None, None, "gx", "gy"), P(None, None, "gx", "gy"), P()),
        check_vma=False,
    )
```

time: 473 us -> 66 us (0.14)
  blocking collectives: 161 us -> 0 us
  other arithmetic: 134 us -> 0 us
  matrix products: 79 us -> 0 us
  Pallas kernels: 0 us -> 61.3 us
  loops' own time: 47.6 us -> 0 us
  starting transfers between devices: 22.8 us -> 0 us
  local copies, waits for them, and re-layouts: 24.8 us -> 3.86 us
    psum x2 -> x0, blocking collectives: 161 us -> none  [the longest x1 81 us: per_device(): lax.psum(inner(basis_flat, applied_flat), ('gx', 'gy')) / cell_count]
    reduce_sum x256 -> x0, other arithmetic: 89.5 us -> none  [the longest x64 38.7 us: one_row(): pivot = jnp.sum(factor_row * picker)]
    dot_general x67 -> x0, matrix products: 79 us -> none  [the longest x64 50.1 us: one_row(): jnp.dot(factor_row[None, :], inverse, precision=lax.Precision.HIGHEST, pr...]
    pallas_call x0 -> x2, Pallas kernels: none -> 61.3 us  [the longest x1 43.6 us: gathered(): pl.pallas_call(gather_kernel, out_shape=(pltpu.VMEM((CELLS, 2 * K, TY), B...]
    another operation x2 -> x0, loops' own time: 47.6 us -> none  [the longest x1 46.9 us: upper_factor(): return lax.fori_loop(0, order, one_column, start)[1]]
    add x129 -> x0, other arithmetic: 34.4 us -> none  [the longest x1 23.8 us: apply_stencil(): result = result + 0.5 * (cond_centre + cond_near) * (centre - neighbour)]
    ppermute x8 -> x0, starting transfers between devices: 22.8 us -> none  [the longest x4 15.7 us: with_halo(): lax.ppermute(tail, axis, [(i, (i + 1) % count) for i in range(ends)])]
    unnamed x13 -> x6, local copies, waits for them, and re-layouts: 13.5 us -> 3.86 us
  transfers between devices with their start and end apart: 8 -> 0, of which waited for: 1 -> 0; matrix products, arithmetic and copies ran while one was open for 39% -> 0% of each run, Pallas kernels for 0% -> 0%
where the time goes in v1:
time: 66 us; the launch traced here: 65.8 us
  Pallas kernels  61.3 us (93%)
  local copies, waits for them, and re-layouts  3.86 us (6%)
    pallas_call x1, Pallas kernels, gathered(): pl.pallas_call(gather_kernel, out_shape=(pltpu.VMEM((CELLS, 2 * K, TY), B...  43.6 us
    pallas_call x1, Pallas kernels, expanded(): pl.pallas_call(expand_kernel, out_shape=(shape, shape, jax.ShapeDtypeStru...  17.7 us
    unnamed x6, local copies, waits for them, and re-layouts  3.86 us

profile of v1, /device:TPU:1, one launch (start us, length us, event | category | flops | bytes accessed | tf_op | source)
XLA Modules:
  0.0 65.8 jit_solution(3212355527646558581)
XLA Ops:
  0.6 0.0 copy-start
  0.6 2.2 %copy-done = f32[64,4,32,128]{3,2,1,0:T(8,128)S(1)} copy-done((f32[64,4,32,128]{3,2,1,0:T(8,128)S(1)}, f32[64,4,32,128]{3,2,1,0:T(8,128)}, u32[]{:S(2)}) %copy-start) | copy-done | bytes 4194328
  2.8 0.0 copy-start.1
  2.8 0.8 %copy-done.1 = f32[4,32,128]{2,1,0:T(8,128)S(1)} copy-done((f32[4,32,128]{2,1,0:T(8,128)S(1)}, f32[4,32,128]{2,1,0:T(8,128)}, u32[]{:S(2)}) %copy-start.1) | copy-done | bytes 65560
  3.7 0.0 copy-start.2
  3.7 0.8 %copy-done.2 = f32[4,32,128]{2,1,0:T(8,128)S(1)} copy-done((f32[4,32,128]{2,1,0:T(8,128)S(1)}, f32[4,32,128]{2,1,0:T(8,128)}, u32[]{:S(2)}) %copy-start.2) | copy-done | bytes 65560
  4.5 43.6 %shard_map.58 = (bf16[128,128,128]{2,1,0:T(8,128)(2,1)S(1)}, bf16[128,128,128]{2,1,0:T(8,128)(2,1)S(1)}, bf16[64,256]{1,0:T(8,128)(2,1)S(1)}, f32[64,64]{1,0:T(8,128)S(1)}) custom-call(f32[64,128,128]{2,1,0:T(8,128)S(1)} %bitcast.5, f32[128,128]{1,0:T(8,128)S(1)} %bitcast.6, f32[128,128]{1,0:T(8,128)S(1)} %bitcast.7), custom_call_target="tpu_custom_call" | custom-call | tf_op jit(solution)/shard_map/pallas_call | solution.py:373
  48.1 17.7 %shard_map.59 = (f32[64,128,128]{2,1,0:T(8,128)}, f32[64,128,128]{2,1,0:T(8,128)}, f32[64,64]{1,0:T(8,128)}) custom-call(bf16[128,128,128]{2,1,0:T(8,128)(2,1)S(1)} %get-tuple-element.10.snap, bf16[128,128,128]{2,1,0:T(8,128)(2,1)S(1)} %get-tuple-element.11.flux, bf16[64,256]{1,0:T(8,128)(2,1)S(1)} %get-tuple-element.12.weights, ...), custom_call_target="tpu_custom_call" | custom-call | tf_op jit(solution)/shard_map/pallas_call | solution.py:454
Async XLA Ops:
  0.6 2.2 %copy-start = (f32[64,4,32,128]{3,2,1,0:T(8,128)S(1)}, f32[64,4,32,128]{3,2,1,0:T(8,128)}, u32[]{:S(2)}) copy-start(f32[64,4,32,128]{3,2,1,0:T(8,128)} %param.3) | copy-start | bytes 12582916
  2.8 0.8 %copy-start.1 = (f32[4,32,128]{2,1,0:T(8,128)S(1)}, f32[4,32,128]{2,1,0:T(8,128)}, u32[]{:S(2)}) copy-start(f32[4,32,128]{2,1,0:T(8,128)} %param.4) | copy-start | bytes 196612
  3.7 0.8 %copy-start.2 = (f32[4,32,128]{2,1,0:T(8,128)S(1)}, f32[4,32,128]{2,1,0:T(8,128)}, u32[]{:S(2)}) copy-start(f32[4,32,128]{2,1,0:T(8,128)} %param.5) | copy-start | bytes 196612

commit v2 on v1

--- a/solution.py
+++ b/solution.py
@@ -15,6 +15,7 @@
 TX = 32
 TY = 128
 CELLS = LAYERS * TX
+PITCH = CELLS + 8
 XY = 16
 Z = 8
 COUNT = 4 * 256 * 4096
@@ -159,10 +160,96 @@
     return whole[:, K:] * (1.0 / jnp.sqrt(pivots))
 
 
+UNROLL0 = 2
+UNROLL1 = 4
+UNROLL2 = 4
+UNROLL3 = 16
+
+
+def edge_pass(l, natural, field, edges):
+    lane = lanes((K, TY))
+
+    def four_rows(turn, carry):
+        kept = [edges[0], edges[1]]
+        for d in range(4):
+            x = turn * 4 + d
+            cell = l * TX + x
+            value = natural[pl.ds(cell, K, stride=PITCH), :]
+            field[x + 1, l] = value
+            turned = pltpu.roll(value, cell, 1)
+            here = (lane == cell) | (lane == lax.rem(cell + TY - 1, TY))
+            kept[d % 2] = jnp.where(here, turned, kept[d % 2])
+        edges[0], edges[1] = kept
+        return carry
+
+    lax.fori_loop(0, TX // 4, four_rows, 0, unroll=UNROLL0)
+
+
+def gram_pass(field, snap, gram_acc):
+    def one_row(x, carry):
+        highs, lows = [], []
+        for l in range(LAYERS):
+            cell = l * TX + x
+            high, low = split(field[x + 1, l])
+            snap[cell, 0:K] = high
+            snap[cell, K : 2 * K] = low
+            highs.append(high)
+            lows.append(low)
+        high = jnp.concatenate(highs, axis=1)
+        low = jnp.concatenate(lows, axis=1)
+        gram_acc[...] += product_nt(jnp.concatenate([high, low], axis=0), high)
+        return carry
+
+    lax.fori_loop(0, TX, one_row, 0, unroll=UNROLL1)
+
+
+def expand_pass(weights, source, held):
+    def two_cells(turn, carry):
+        cell = turn * 2
+        pair = jnp.concatenate([source[cell], source[cell + 1]], axis=1)
+        out = jnp.dot(weights, jnp.concatenate([pair, pair], axis=0), preferred_element_type=F32)
+        held[pl.ds(cell, K, stride=PITCH), :] = out[:, :TY]
+        held[pl.ds(cell + 1, K, stride=PITCH), :] = out[:, TY:]
+        return carry
+
+    lax.fori_loop(0, CELLS // 2, two_cells, 0, unroll=UNROLL3)
+
+
+def second_pass(coefs, field, flat, snap, flux, proj_acc):
+    def two_rows(turn, carry):
+        for d in range(2):
+            x = turn * 2 + d
+            for l in range(LAYERS):
+                cell = l * TX + x
+                coef = [coefs[i, pl.ds(cell, 1), :] for i in range(8)]
+                here = field[x + 1, l]
+                value = coef[0] * here
+                value = value - coef[1] * field[x + 2, l]
+                value = value - coef[2] * field[x, l]
+                if l + 1 < LAYERS:
+                    value = value - coef[3] * field[x + 1, l + 1]
+                if l:
+                    value = value - coef[4] * field[x + 1, l - 1]
+                value = value - coef[5] * pltpu.roll(here, TY - 1, 1)
+                value = value - coef[6] * pltpu.roll(here, 1, 1)
+                value = value - coef[7] * pltpu.roll(flat[d], lax.rem(TY - cell, TY), 1)
+                high, low = split(value)
+                flux[cell, 0:K] = high
+                flux[cell, K : 2 * K] = low
+        cells = [l * TX + turn * 2 + d for d in range(2) for l in range(LAYERS)]
+        proj_acc[...] += product_nt(
+            jnp.concatenate([snap[cell] for cell in cells], axis=1),
+            jnp.concatenate([flux[cell] for cell in cells], axis=1),
+        )
+        return carry
+
+    lax.fori_loop(0, TX // 2, two_rows, 0, unroll=UNROLL2)
+
+
 def gather_kernel(
     snap_any, cond_any, stor_any,
-    snap_out, flux_out, weights_out, reduced_out,
-    natural, field, cond, stor, padded, coefs, edges, flat,
+    basis_held, applied_held, reduced_out,
+    snap, flux, natural, field, cond, stor, padded, coefs, edges, flat,
     gram_acc, proj_acc,
     side_send, side_cond_send, side_cond, end_send, end_got,
     g_packed, g_pair, g_plane, g_column, g_whole,
@@ -174,7 +261,7 @@
     gram_total = Total(place, g_packed, g_pair, g_plane, g_column, g_whole, g_send, g_recv)
     proj_total = Total(place, m_packed, m_pair, m_plane, m_column, m_whole, m_send, m_recv)
 
-    natural3 = natural.reshape(K, CELLS, TY)
+    natural3 = natural.reshape(K, PITCH, TY)
     loads = []
     for l in range(LAYERS):
         part = pl.ds(l * TX, TX)
@@ -196,37 +283,13 @@
 
     gram_acc[...] = jnp.zeros_like(gram_acc)
     proj_acc[...] = jnp.zeros_like(proj_acc)
-    lane = lanes((K, TY))
-
     for l in range(LAYERS):
         loads[l].wait()
-
-        def four_rows(turn, carry):
-            highs, lows = [], []
-            for d in range(4):
-                x = turn * 4 + d
-                cell = l * TX + x
-                value = natural[pl.ds(cell, K, stride=CELLS), :]
-                field[x + 1, l] = value
-                high, low = split(value)
-                snap_out[cell, 0:K] = high
-                snap_out[cell, K : 2 * K] = low
-                turned = pltpu.roll(value, cell, 1)
-                here = (lane == cell) | (lane == lax.rem(cell + TY - 1, TY))
-                edges[d % 2] = jnp.where(here, turned, edges[d % 2])
-                highs.append(high)
-                lows.append(low)
-            high = jnp.concatenate(highs, axis=1)
-            low = jnp.concatenate(lows, axis=1)
-            gram_acc[...] += product_nt(jnp.concatenate([high, low], axis=0), high)
-            return carry
-
-        lax.fori_loop(0, TX // 4, four_rows, 0)
+        edge_pass(l, natural, field, edges)
 
     loads[LAYERS].wait()
-    loads[LAYERS + 1].wait()
-
-    even = lax.rem(lane, 2) == 0
+
+    even = lax.rem(lanes((K, TY)), 2) == 0
     end_send[0, 0:K] = jnp.where(even, edges[0], edges[1])
     end_send[1, 0:K] = jnp.where(even, edges[1], edges[0])
     lane8 = lanes((8, TY))
@@ -242,12 +305,6 @@
         side_cond_send[0, l : l + 1] = cond[l * TX : l * TX + 1, :]
         side_cond_send[1, l : l + 1] = cond[l * TX + TX - 1 : l * TX + TX, :]
 
-    cross = gram_acc[K : 2 * K]
-    gram_part = gram_acc[0:K] + (cross + cross.T)
-
-    pl.semaphore_wait(barrier, len(partners))
-    gram_total.start_pair(gram_part)
-
     def halo(src, dst, which, device):
         copy = pltpu.make_async_remote_copy(
             src_ref=src, dst_ref=dst, send_sem=halo_send.at[which], recv_sem=halo_recv.at[which],
@@ -256,17 +313,26 @@
         copy.start()
         return copy
 
-    halos = [
+    pl.semaphore_wait(barrier, len(partners))
+    cond_halos = [
         halo(side_cond_send.at[0], side_cond.at[1], 0, x_left),
         halo(side_cond_send.at[1], side_cond.at[0], 1, x_right),
         halo(end_send.at[0], end_got.at[1], 2, y_left),
         halo(end_send.at[1], end_got.at[0], 3, y_right),
+    ]
+    field_halos = [
         halo(field.at[1], field.at[TX + 1], 4, x_left),
         halo(field.at[TX], field.at[0], 5, x_right),
     ]
+    halos = cond_halos + field_halos
+
+    gram_pass(field, snap, gram_acc)
+    cross = gram_acc[K : 2 * K]
+    gram_total.start_pair(gram_acc[0:K] + (cross + cross.T))
     gram_total.start_plane()
 
-    for copy in halos:
+    loads[LAYERS + 1].wait()
+    for copy in cond_halos:
         copy.wait_recv()
 
     first_x, last_x = gx == 0, gx == 7
@@ -309,46 +375,22 @@
     flat[0] = jnp.where(even, from_left, from_right)
     flat[1] = jnp.where(even, from_right, from_left)
 
-    def two_rows(turn, carry):
-        for d in range(2):
-            x = turn * 2 + d
-            for l in range(LAYERS):
-                cell = l * TX + x
-                coef = [coefs[i, pl.ds(cell, 1), :] for i in range(8)]
-                here = field[x + 1, l]
-                value = coef[0] * here
-                value = value - coef[1] * field[x + 2, l]
-                value = value - coef[2] * field[x, l]
-                if l + 1 < LAYERS:
-                    value = value - coef[3] * field[x + 1, l + 1]
-                if l:
-                    value = value - coef[4] * field[x + 1, l - 1]
-                value = value - coef[5] * pltpu.roll(here, TY - 1, 1)
-                value = value - coef[6] * pltpu.roll(here, 1, 1)
-                value = value - coef[7] * pltpu.roll(flat[d], lax.rem(TY - cell, TY), 1)
-                high, low = split(value)
-                flux_out[cell, 0:K] = high
-                flux_out[cell, K : 2 * K] = low
-        cells = [l * TX + turn * 2 + d for d in range(2) for l in range(LAYERS)]
-        proj_acc[...] += product_nt(
-            jnp.concatenate([snap_out[cell] for cell in cells], axis=1),
-            jnp.concatenate([flux_out[cell] for cell in cells], axis=1),
-        )
-        return carry
-
-    lax.fori_loop(0, TX // 4, two_rows, 0)
+    for copy in field_halos:
+        copy.wait_recv()
+    second_pass(coefs, field, flat, snap, flux, proj_acc)
     gram_total.start_column()
-    lax.fori_loop(TX // 4, TX // 2, two_rows, 0)
     proj_part = (
         proj_acc[0:K, 0:K] + (proj_acc[K : 2 * K, 0:K] + proj_acc[0:K, K : 2 * K]) + proj_acc[K : 2 * K, K : 2 * K]
     )
     proj_total.start_pair(proj_part)
     proj_total.start_plane()
     gram_total.start_whole()
+    proj_total.start_column()
     weights = eliminated(gram_total.result() * (1.0 / COUNT))
     high, low = split(weights)
-    weights_out[...] = jnp.concatenate([high, high, low, low], axis=1)
-    proj_total.start_column()
+    wide = jnp.concatenate([high, high, low, low], axis=1)
+    expand_pass(wide, snap, basis_held)
+    expand_pass(wide, flux, applied_held)
     proj_total.start_whole()
     exact = dict(precision=lax.Precision.HIGHEST, preferred_element_type=F32)
     half = jnp.dot(weights, proj_total.result(), **exact)
@@ -373,15 +415,16 @@
     return pl.pallas_call(
         gather_kernel,
         out_shape=(
-            pltpu.VMEM((CELLS, 2 * K, TY), BF16),
-            pltpu.VMEM((CELLS, 2 * K, TY), BF16),
-            pltpu.VMEM((K, 4 * K), BF16),
+            pltpu.VMEM((K * PITCH, TY), F32),
+            pltpu.VMEM((K * PITCH, TY), F32),
             pltpu.VMEM((K, K), F32),
         ),
         in_specs=[any_spec] * 3,
-        out_specs=(vmem_spec,) * 4,
+        out_specs=(vmem_spec,) * 3,
         scratch_shapes=[
-            pltpu.VMEM((K * CELLS, TY), F32),
+            pltpu.VMEM((CELLS, 2 * K, TY), BF16),
+            pltpu.VMEM((CELLS, 2 * K, TY), BF16),
+            pltpu.VMEM((K * PITCH, TY), F32),
             pltpu.VMEM((TX + 2, LAYERS, K, TY), F32),
             pltpu.VMEM((CELLS, TY), F32),
             pltpu.VMEM((CELLS, TY), F32),
@@ -410,63 +453,46 @@
             collective_id=0, has_side_effects=True, vmem_limit_bytes=40 * 2**20
         ),
     )(
-        snapshots.reshape(K, CELLS, TY),
-        conductivity.reshape(CELLS, TY),
-        storage.reshape(CELLS, TY),
+        pltpu.with_memory_space_constraint(snapshots.reshape(K, CELLS, TY), pltpu.HBM),
+        pltpu.with_memory_space_constraint(conductivity.reshape(CELLS, TY), pltpu.HBM),
+        pltpu.with_memory_space_constraint(storage.reshape(CELLS, TY), pltpu.HBM),
     )
 
 
-PART = 16
-
-
-def expand_kernel(snap, flux, weights, reduced_in, basis, applied, reduced, basis_held, applied_held, sems):
-    reduced[...] = reduced_in[...]
+PARTS = 4
+
+
+def write_kernel(basis_held, applied_held, reduced_in, basis, applied, reduced, sems):
     copies = []
-    for part in range(CELLS // PART):
-
-        def two_cells(turn, carry):
-            cell = part * PART + turn * 2
-            for source, held in ((snap, basis_held), (flux, applied_held)):
-                pair = jnp.concatenate([source[cell], source[cell + 1]], axis=1)
-                out = jnp.dot(
-                    weights[...], jnp.concatenate([pair, pair], axis=0), preferred_element_type=F32
-                )
-                held[pl.ds(cell, K, stride=CELLS), :] = out[:, :TY]
-                held[pl.ds(cell + 1, K, stride=CELLS), :] = out[:, TY:]
-            return carry
-
-        lax.fori_loop(0, PART // 2, two_cells, 0)
-        span = pl.ds(part * PART, PART)
+    for part in range(PARTS):
+        span = pl.ds(part * (K // PARTS), K // PARTS)
         for which, (held, target) in enumerate(((basis_held, basis), (applied_held, applied))):
             copy = pltpu.make_async_copy(
-                held.reshape(K, CELLS, TY).at[:, span], target.at[:, span], sems.at[which, part]
+                held.reshape(K, PITCH, TY).at[span, 0:CELLS], target.at[span], sems.at[which, part]
             )
             copy.start()
             copies.append(copy)
+    reduced[...] = reduced_in[...]
     for copy in copies:
         copy.wait()
 
 
-def expanded(snap, flux, weights, reduced):
+def written(basis_held, applied_held, reduced):
     vmem_spec = pl.BlockSpec(memory_space=pltpu.VMEM)
-    any_spec = pl.BlockSpec(memory_space=pltpu.HBM)
+    hbm_spec = pl.BlockSpec(memory_space=pltpu.HBM)
     shape = jax.ShapeDtypeStruct((K, CELLS, TY), F32)
     return pl.pallas_call(
-        expand_kernel,
+        write_kernel,
         out_shape=(shape, shape, jax.ShapeDtypeStruct((K, K), F32)),
-        in_specs=[vmem_spec] * 4,
-        out_specs=(any_spec, any_spec, vmem_spec),
-        scratch_shapes=[
-            pltpu.VMEM((K * CELLS, TY), F32),
-            pltpu.VMEM((K * CELLS, TY), F32),
-            pltpu.SemaphoreType.DMA((2, CELLS // PART)),
-        ],
-        compiler_params=pltpu.CompilerParams(vmem_limit_bytes=40 * 2**20),
-    )(snap, flux, weights, reduced)
+        in_specs=[vmem_spec] * 3,
+        out_specs=(hbm_spec, hbm_spec, vmem_spec),
+        scratch_shapes=[pltpu.SemaphoreType.DMA((2, PARTS))],
+        compiler_params=pltpu.CompilerParams(vmem_limit_bytes=16 * 2**20),
+    )(basis_held, applied_held, reduced)
 
 
 def per_device(snapshots, conductivity, storage):
-    basis, applied, reduced = expanded(*gathered(snapshots, conductivity, storage))
+    basis, applied, reduced = written(*gathered(snapshots, conductivity, storage))
     return (basis.reshape(snapshots.shape), applied.reshape(snapshots.shape), reduced)
 
 

time: 66 us -> 38.7 us (0.59)
  Pallas kernels: 61.3 us -> 37.9 us
  local copies, waits for them, and re-layouts: 3.86 us -> 0 us
    pallas_call x2, Pallas kernels: 61.3 us -> 37.9 us  [the longest x1 34 us: gathered(): pl.pallas_call(gather_kernel, out_shape=(pltpu.VMEM((K * PITCH, TY), F32)...]
    unnamed x6 -> x0, local copies, waits for them, and re-layouts: 3.86 us -> none
where the time goes in v2:
time: 38.7 us; the launch traced here: 38.6 us
  Pallas kernels  37.9 us (98%)
  between operations  0.64 us (2%)
    pallas_call x1, Pallas kernels, gathered(): pl.pallas_call(gather_kernel, out_shape=(pltpu.VMEM((K * PITCH, TY), F32)...  34 us
    pallas_call x1, Pallas kernels, written(): pl.pallas_call(write_kernel, out_shape=(shape, shape, jax.ShapeDtypeStruc...  3.98 us

profile of v2, /device:TPU:1, one launch (start us, length us, event | category | flops | bytes accessed | tf_op | source)
XLA Modules:
  0.0 38.6 jit_solution(5470762264752768653)
XLA Ops:
  0.6 34.0 %shard_map.58 = (f32[8704,128]{1,0:T(8,128)S(1)}, f32[8704,128]{1,0:T(8,128)S(1)}, f32[64,64]{1,0:T(8,128)S(1)}) custom-call(f32[64,128,128]{2,1,0:T(8,128)} %bitcast.5, f32[128,128]{1,0:T(8,128)} %bitcast.6, f32[128,128]{1,0:T(8,128)} %bitcast.7), custom_call_target="tpu_custom_call" | custom-call | tf_op jit(solution)/shard_map/pallas_call | solution.py:415
  34.6 4.0 %shard_map.59 = (f32[64,128,128]{2,1,0:T(8,128)}, f32[64,128,128]{2,1,0:T(8,128)}, f32[64,64]{1,0:T(8,128)}) custom-call(f32[8704,128]{1,0:T(8,128)S(1)} %get-tuple-element.9.basis_held, f32[8704,128]{1,0:T(8,128)S(1)} %get-tuple-element.10.applied_held, f32[64,64]{1,0:T(8,128)S(1)} %get-tuple-element.11.reduced_in), custom_call_target="tpu_custom_call" | custom-call | tf_op jit(solution)/shard_map/pallas_call | solution.py:484

commit v3 on v2

--- a/solution.py
+++ b/solution.py
@@ -160,10 +160,10 @@
     return whole[:, K:] * (1.0 / jnp.sqrt(pivots))
 
 
-UNROLL0 = 2
-UNROLL1 = 4
-UNROLL2 = 4
-UNROLL3 = 16
+UNROLL0 = 8
+UNROLL1 = 8
+UNROLL2 = 5
+UNROLL3 = 32
 
 
 def edge_pass(l, natural, field, edges):
@@ -215,43 +215,76 @@
     lax.fori_loop(0, CELLS // 2, two_cells, 0, unroll=UNROLL3)
 
 
-def second_pass(coefs, field, flat, snap, flux, proj_acc):
+def local_coefficients(cond, stor, coefs):
+    lane, row = lanes((8, TY)), rows((8, TY))
+    for l in range(LAYERS):
+        for b in range(TX // 8):
+            at = l * TX + 8 * b
+            here = cond[at : at + 8, :]
+
+            def face(first):
+                return 0.5 * (here + cond[first : first + 8, :])
+
+            if 8 * b + 8 < TX:
+                x_up = face(at + 1)
+            else:
+                x_up = jnp.where(row == 7, 0.0, 0.5 * (here + pltpu.roll(here, 7, 0)))
+            if b:
+                x_down = face(at - 1)
+            else:
+                x_down = jnp.where(row == 0, 0.0, 0.5 * (here + pltpu.roll(here, 1, 0)))
+            l_up = face(at + TX) if l + 1 < LAYERS else 0.5 * here
+            l_down = face(at - TX) if l else 0.5 * here
+            y_up = jnp.where(lane == TY - 1, 0.0, 0.5 * (here + pltpu.roll(here, TY - 1, 1)))
+            y_down = jnp.where(lane == 0, 0.0, 0.5 * (here + pltpu.roll(here, 1, 1)))
+            centre = stor[at : at + 8, :] + x_up + x_down + l_up + l_down + y_up + y_down
+            for i, value in enumerate((centre, x_up, x_down, l_up, l_down, y_up, y_down)):
+                coefs[i, at : at + 8] = value
+
+
+def flux_rows(xs, coefs, field, snap, flux, proj_acc, x_faces=()):
+    for at, x in enumerate(xs):
+        for l in range(LAYERS):
+            cell = l * TX + x
+            coef = [coefs[i, pl.ds(cell, 1), :] for i in range(7)]
+            here = field[x + 1, l]
+            value = coef[0] * here
+            if not x_faces or at == 0:
+                value = value - coef[1] * field[x + 2, l]
+            if not x_faces or at == 1:
+                value = value - coef[2] * field[x, l]
+            if l + 1 < LAYERS:
+                value = value - coef[3] * field[x + 1, l + 1]
+            if l:
+                value = value - coef[4] * field[x + 1, l - 1]
+            value = value - coef[5] * pltpu.roll(here, TY - 1, 1)
+            value = value - coef[6] * pltpu.roll(here, 1, 1)
+            if x_faces:
+                value = value + x_faces[at](l, here)
+            high, low = split(value)
+            flux[cell, 0:K] = high
+            flux[cell, K : 2 * K] = low
+    cells = [l * TX + x for x in xs for l in range(LAYERS)]
+    proj_acc[...] += product_nt(
+        jnp.concatenate([snap[cell] for cell in cells], axis=1),
+        jnp.concatenate([flux[cell] for cell in cells], axis=1),
+    )
+
+
+def second_pass(coefs, field, snap, flux, proj_acc):
     def two_rows(turn, carry):
-        for d in range(2):
-            x = turn * 2 + d
-            for l in range(LAYERS):
-                cell = l * TX + x
-                coef = [coefs[i, pl.ds(cell, 1), :] for i in range(8)]
-                here = field[x + 1, l]
-                value = coef[0] * here
-                value = value - coef[1] * field[x + 2, l]
-                value = value - coef[2] * field[x, l]
-                if l + 1 < LAYERS:
-                    value = value - coef[3] * field[x + 1, l + 1]
-                if l:
-                    value = value - coef[4] * field[x + 1, l - 1]
-                value = value - coef[5] * pltpu.roll(here, TY - 1, 1)
-                value = value - coef[6] * pltpu.roll(here, 1, 1)
-                value = value - coef[7] * pltpu.roll(flat[d], lax.rem(TY - cell, TY), 1)
-                high, low = split(value)
-                flux[cell, 0:K] = high
-                flux[cell, K : 2 * K] = low
-        cells = [l * TX + turn * 2 + d for d in range(2) for l in range(LAYERS)]
-        proj_acc[...] += product_nt(
-            jnp.concatenate([snap[cell] for cell in cells], axis=1),
-            jnp.concatenate([flux[cell] for cell in cells], axis=1),
-        )
+        flux_rows((1 + 2 * turn, 2 + 2 * turn), coefs, field, snap, flux, proj_acc)
         return carry
 
-    lax.fori_loop(0, TX // 2, two_rows, 0, unroll=UNROLL2)
+    lax.fori_loop(0, TX // 2 - 1, two_rows, 0, unroll=UNROLL2)
 
 
 def gather_kernel(
     snap_any, cond_any, stor_any,
-    basis_held, applied_held, reduced_out,
-    snap, flux, natural, field, cond, stor, padded, coefs, edges, flat,
+    basis_held, flux, wide_out, rim_out, weights_out, proj_out,
+    snap, natural, field, cond, stor, coefs, edges,
     gram_acc, proj_acc,
-    side_send, side_cond_send, side_cond, end_send, end_got,
+    side_send, side_got, end_send, end_got,
     g_packed, g_pair, g_plane, g_column, g_whole,
     m_packed, m_pair, m_plane, m_column, m_whole,
     load_sem, halo_send, halo_recv, g_send, g_recv, m_send, m_recv,
@@ -262,12 +295,13 @@
     proj_total = Total(place, m_packed, m_pair, m_plane, m_column, m_whole, m_send, m_recv)
 
     natural3 = natural.reshape(K, PITCH, TY)
-    loads = []
+    loads = [
+        pltpu.make_async_copy(cond_any, cond, load_sem.at[LAYERS]),
+        pltpu.make_async_copy(stor_any, stor, load_sem.at[LAYERS + 1]),
+    ]
     for l in range(LAYERS):
         part = pl.ds(l * TX, TX)
         loads.append(pltpu.make_async_copy(snap_any.at[:, part], natural3.at[:, part], load_sem.at[l]))
-    loads.append(pltpu.make_async_copy(cond_any, cond, load_sem.at[LAYERS]))
-    loads.append(pltpu.make_async_copy(stor_any, stor, load_sem.at[LAYERS + 1]))
     for load in loads:
         load.start()
 
@@ -283,27 +317,25 @@
 
     gram_acc[...] = jnp.zeros_like(gram_acc)
     proj_acc[...] = jnp.zeros_like(proj_acc)
+    loads[0].wait()
+    loads[1].wait()
+    local_coefficients(cond, stor, coefs)
+
+    side_send[...] = jnp.zeros_like(side_send)
     for l in range(LAYERS):
-        loads[l].wait()
+        side_send[0, l : l + 1] = cond[l * TX : l * TX + 1, :]
+        side_send[1, l : l + 1] = cond[l * TX + TX - 1 : l * TX + TX, :]
+    turned = cond[...].T
+    end_send[0, K : K + 8] = turned[0:8]
+    end_send[1, K : K + 8] = turned[TY - 8 : TY]
+
+    for l in range(LAYERS):
+        loads[2 + l].wait()
         edge_pass(l, natural, field, edges)
-
-    loads[LAYERS].wait()
 
     even = lax.rem(lanes((K, TY)), 2) == 0
     end_send[0, 0:K] = jnp.where(even, edges[0], edges[1])
-    end_send[1, 0:K] = jnp.where(even, edges[1], edges[0])
-    lane8 = lanes((8, TY))
-    ends = jnp.zeros((8, TY), F32)
-    for i in range(16):
-        value = cond[8 * i : 8 * i + 8, :]
-        ends = jnp.where(lane8 == i, pltpu.roll(value, i, 1) if i else value, ends)
-        ends = jnp.where(lane8 == 16 + i, pltpu.roll(value, 17 + i, 1), ends)
-    end_send[0, K : K + 8] = ends
-    end_send[1, K : K + 8] = ends
-    side_cond_send[...] = jnp.zeros_like(side_cond_send)
-    for l in range(LAYERS):
-        side_cond_send[0, l : l + 1] = cond[l * TX : l * TX + 1, :]
-        side_cond_send[1, l : l + 1] = cond[l * TX + TX - 1 : l * TX + TX, :]
+    end_send[1, 0:K] = pltpu.roll(jnp.where(even, edges[1], edges[0]), 1, 1)
 
     def halo(src, dst, which, device):
         copy = pltpu.make_async_remote_copy(
@@ -314,88 +346,78 @@
         return copy
 
     pl.semaphore_wait(barrier, len(partners))
-    cond_halos = [
-        halo(side_cond_send.at[0], side_cond.at[1], 0, x_left),
-        halo(side_cond_send.at[1], side_cond.at[0], 1, x_right),
-        halo(end_send.at[0], end_got.at[1], 2, y_left),
-        halo(end_send.at[1], end_got.at[0], 3, y_right),
+    x_halos = [
+        halo(field.at[1], field.at[TX + 1], 0, x_left),
+        halo(field.at[TX], field.at[0], 1, x_right),
+        halo(side_send.at[0], side_got.at[1], 2, x_left),
+        halo(side_send.at[1], side_got.at[0], 3, x_right),
     ]
-    field_halos = [
-        halo(field.at[1], field.at[TX + 1], 4, x_left),
-        halo(field.at[TX], field.at[0], 5, x_right),
+    y_halos = [
+        halo(end_send.at[0], end_got.at[1], 4, y_left),
+        halo(end_send.at[1], end_got.at[0], 5, y_right),
     ]
-    halos = cond_halos + field_halos
 
     gram_pass(field, snap, gram_acc)
     cross = gram_acc[K : 2 * K]
     gram_total.start_pair(gram_acc[0:K] + (cross + cross.T))
     gram_total.start_plane()
 
-    loads[LAYERS + 1].wait()
-    for copy in cond_halos:
+    second_pass(coefs, field, snap, flux, proj_acc)
+
+    for copy in x_halos:
         copy.wait_recv()
 
-    first_x, last_x = gx == 0, gx == 7
-    first_y, last_y = gy == 0, gy == 31
-    for l in range(LAYERS):
-        padded[l, 8 : 8 + TX] = cond[l * TX : l * TX + TX, :]
-        padded[l, 7:8] = jnp.where(first_x, 0.0, side_cond[0, l : l + 1])
-        padded[l, 8 + TX : 9 + TX] = jnp.where(last_x, 0.0, side_cond[1, l : l + 1])
-    row8 = rows((8, TY))
-    for l in range(LAYERS):
-        for b in range(TX // 8):
-            at = l * TX + 8 * b
-            i = at // 8
-            here = padded[l, 8 + 8 * b : 16 + 8 * b]
-            x_up = 0.5 * (here + padded[l, 9 + 8 * b : 17 + 8 * b])
-            x_down = 0.5 * (here + padded[l, 7 + 8 * b : 15 + 8 * b])
-            l_up = 0.5 * (here + padded[l + 1, 8 + 8 * b : 16 + 8 * b]) if l + 1 < LAYERS else 0.5 * here
-            l_down = 0.5 * (here + padded[l - 1, 8 + 8 * b : 16 + 8 * b]) if l else 0.5 * here
-            left = jnp.where(first_y, 0.0, pltpu.roll(end_got[0, K : K + 8], TY - 16 - i, 1))
-            right = jnp.where(last_y, 0.0, pltpu.roll(end_got[1, K : K + 8], TY - 1 - i, 1))
-            y_down = 0.5 * (here + jnp.where(lane8 == 0, left, pltpu.roll(here, 1, 1)))
-            y_up = 0.5 * (here + jnp.where(lane8 == TY - 1, right, pltpu.roll(here, TY - 1, 1)))
-            centre = stor[at : at + 8, :] + x_up + x_down + l_up + l_down + y_up + y_down
-            span = slice(at, at + 8)
-            coefs[0, span] = centre
-            coefs[1, span] = jnp.where(last_x & (row8 == 7), 0.0, x_up) if b == TX // 8 - 1 else x_up
-            coefs[2, span] = jnp.where(first_x & (row8 == 0), 0.0, x_down) if b == 0 else x_down
-            coefs[3, span] = l_up
-            coefs[4, span] = l_down
-            coefs[5, span] = jnp.where(lane8 == TY - 1, 0.0, y_up)
-            coefs[6, span] = jnp.where(lane8 == 0, 0.0, y_down)
-            coefs[7, span] = jnp.where(
-                lane8 == 0,
-                jnp.where(first_y, 0.0, y_down),
-                jnp.where(lane8 == TY - 1, jnp.where(last_y, 0.0, y_up), 0.0),
-            )
-
-    from_left = pltpu.roll(end_got[0, 0:K], 1, 1)
-    from_right = pltpu.roll(end_got[1, 0:K], TY - 1, 1)
-    flat[0] = jnp.where(even, from_left, from_right)
-    flat[1] = jnp.where(even, from_right, from_left)
-
-    for copy in field_halos:
+    def x_face(side, row, at_rim):
+        inside = jnp.where(at_rim, 0.0, 1.0)
+
+        def added(l, here):
+            own = cond[l * TX + row : l * TX + row + 1, :]
+            face = 0.5 * (own + inside * side_got[side, l : l + 1])
+            return face * (here - inside * field[0 if side == 0 else TX + 1, l])
+
+        return added
+
+    flux_rows(
+        (0, TX - 1), coefs, field, snap, flux, proj_acc,
+        (x_face(0, 0, gx == 0), x_face(1, TX - 1, gx == 7)),
+    )
+
+    for copy in y_halos:
         copy.wait_recv()
-    second_pass(coefs, field, flat, snap, flux, proj_acc)
-    gram_total.start_column()
-    proj_part = (
+    left_in = jnp.where(gy == 0, 0.0, 1.0)
+    right_in = jnp.where(gy == 31, 0.0, 1.0)
+    left_face = 0.5 * (end_send[0, K : K + 1] + left_in * end_got[0, K + 7 : K + 8])
+    right_face = 0.5 * (end_send[1, K + 7 : K + 8] + right_in * end_got[1, K : K + 1])
+    rim = jnp.concatenate(
+        [
+            left_face * (end_send[0, 0:K] - left_in * end_got[0, 0:K]),
+            right_face * (end_send[1, 0:K] - right_in * end_got[1, 0:K]),
+        ],
+        axis=1,
+    )
+    exact = dict(precision=lax.Precision.HIGHEST, preferred_element_type=F32)
+    ends = jnp.concatenate([end_send[0, 0:K], end_send[1, 0:K]], axis=1)
+    proj_part = lax.dot_general(ends, rim, (((1,), (1,)), ((), ())), **exact) + (
         proj_acc[0:K, 0:K] + (proj_acc[K : 2 * K, 0:K] + proj_acc[0:K, K : 2 * K]) + proj_acc[K : 2 * K, K : 2 * K]
     )
     proj_total.start_pair(proj_part)
     proj_total.start_plane()
+    gram_total.start_column()
     gram_total.start_whole()
     proj_total.start_column()
     weights = eliminated(gram_total.result() * (1.0 / COUNT))
+    weights_out[...] = weights
     high, low = split(weights)
     wide = jnp.concatenate([high, high, low, low], axis=1)
+    wide_out[...] = wide
+    rim = jnp.dot(weights, rim, **exact)
+    left, right = rim[:, :TY], pltpu.roll(rim[:, TY:], TY - 1, 1)
+    rim_out[0] = jnp.where(even, left, right)
+    rim_out[1] = jnp.where(even, right, left)
+    proj_total.start_whole()
     expand_pass(wide, snap, basis_held)
-    expand_pass(wide, flux, applied_held)
-    proj_total.start_whole()
-    exact = dict(precision=lax.Precision.HIGHEST, preferred_element_type=F32)
-    half = jnp.dot(weights, proj_total.result(), **exact)
-    reduced_out[...] = lax.dot_general(half, weights, (((1,), (1,)), ((), ())), **exact) * (1.0 / COUNT)
-    for copy in halos:
+    proj_out[...] = proj_total.result()
+    for copy in x_halos + y_halos:
         copy.wait_send()
     gram_total.drain()
     proj_total.drain()
@@ -416,25 +438,24 @@
         gather_kernel,
         out_shape=(
             pltpu.VMEM((K * PITCH, TY), F32),
-            pltpu.VMEM((K * PITCH, TY), F32),
+            pltpu.VMEM((CELLS, 2 * K, TY), BF16),
+            pltpu.VMEM((K, 4 * K), BF16),
+            pltpu.VMEM((2, K, TY), F32),
+            pltpu.VMEM((K, K), F32),
             pltpu.VMEM((K, K), F32),
         ),
         in_specs=[any_spec] * 3,
-        out_specs=(vmem_spec,) * 3,
+        out_specs=(vmem_spec,) * 6,
         scratch_shapes=[
-            pltpu.VMEM((CELLS, 2 * K, TY), BF16),
             pltpu.VMEM((CELLS, 2 * K, TY), BF16),
             pltpu.VMEM((K * PITCH, TY), F32),
             pltpu.VMEM((TX + 2, LAYERS, K, TY), F32),
             pltpu.VMEM((CELLS, TY), F32),
             pltpu.VMEM((CELLS, TY), F32),
-            pltpu.VMEM((LAYERS, TX + 16, TY), F32),
-            pltpu.VMEM((8, CELLS, TY), F32),
-            pltpu.VMEM((2, K, TY), F32),
+            pltpu.VMEM((7, CELLS, TY), F32),
             pltpu.VMEM((2, K, TY), F32),
             pltpu.VMEM((2 * K, K), F32),
             pltpu.VMEM((2 * K, 2 * K), F32),
-            pltpu.VMEM((LAYERS // 2, 8, TY), F32),
             pltpu.VMEM((2, 8, TY), F32),
             pltpu.VMEM((2, 8, TY), F32),
             pltpu.VMEM((2, K + 8, TY), F32),
@@ -459,36 +480,67 @@
     )
 
 
-PARTS = 4
-
-
-def write_kernel(basis_held, applied_held, reduced_in, basis, applied, reduced, sems):
+PART = 16
+BASIS_PARTS = 4
+
+
+def write_kernel(
+    basis_held, flux, wide, rim, weights, proj, basis, applied, reduced, applied_held, reduced_held, sems
+):
     copies = []
-    for part in range(PARTS):
-        span = pl.ds(part * (K // PARTS), K // PARTS)
-        for which, (held, target) in enumerate(((basis_held, basis), (applied_held, applied))):
-            copy = pltpu.make_async_copy(
-                held.reshape(K, PITCH, TY).at[span, 0:CELLS], target.at[span], sems.at[which, part]
+
+    def out(src, dst):
+        copy = pltpu.make_async_copy(src, dst, sems.at[len(copies)])
+        copy.start()
+        copies.append(copy)
+
+    for part in range(BASIS_PARTS):
+        span = pl.ds(part * (K // BASIS_PARTS), K // BASIS_PARTS)
+        out(basis_held.reshape(K, PITCH, TY).at[span, 0:CELLS], basis.at[span])
+    lane = lanes((K, TY))
+    at_end = (lane == 0) | (lane == TY - 1)
+    for part in range(CELLS // PART):
+
+        def two_cells(turn, carry):
+            cell = part * PART + turn * 2
+            pair = jnp.concatenate([flux[cell], flux[cell + 1]], axis=1)
+            both = jnp.dot(
+                wide[...], jnp.concatenate([pair, pair], axis=0), preferred_element_type=F32
             )
-            copy.start()
-            copies.append(copy)
-    reduced[...] = reduced_in[...]
+            for d in range(2):
+                ends = pltpu.roll(rim[d], lax.rem(TY - d - cell + TY, TY), 1)
+                applied_held[pl.ds(cell + d, K, stride=PITCH), :] = both[
+                    :, d * TY : (d + 1) * TY
+                ] + jnp.where(at_end, ends, 0.0)
+            return carry
+
+        lax.fori_loop(0, PART // 2, two_cells, 0, unroll=True)
+        span = pl.ds(part * PART, PART)
+        out(applied_held.reshape(K, PITCH, TY).at[:, span], applied.at[:, span])
+    exact = dict(precision=lax.Precision.HIGHEST, preferred_element_type=F32)
+    half = jnp.dot(weights[...], proj[...], **exact)
+    reduced_held[...] = lax.dot_general(half, weights[...], (((1,), (1,)), ((), ())), **exact) * (1.0 / COUNT)
+    out(reduced_held, reduced)
     for copy in copies:
         copy.wait()
 
 
-def written(basis_held, applied_held, reduced):
+def written(*held):
     vmem_spec = pl.BlockSpec(memory_space=pltpu.VMEM)
     hbm_spec = pl.BlockSpec(memory_space=pltpu.HBM)
     shape = jax.ShapeDtypeStruct((K, CELLS, TY), F32)
     return pl.pallas_call(
         write_kernel,
         out_shape=(shape, shape, jax.ShapeDtypeStruct((K, K), F32)),
-        in_specs=[vmem_spec] * 3,
-        out_specs=(hbm_spec, hbm_spec, vmem_spec),
-        scratch_shapes=[pltpu.SemaphoreType.DMA((2, PARTS))],
-        compiler_params=pltpu.CompilerParams(vmem_limit_bytes=16 * 2**20),
-    )(basis_held, applied_held, reduced)
+        in_specs=[vmem_spec] * 6,
+        out_specs=(hbm_spec, hbm_spec, hbm_spec),
+        scratch_shapes=[
+            pltpu.VMEM((K * PITCH, TY), F32),
+            pltpu.VMEM((K, K), F32),
+            pltpu.SemaphoreType.DMA((BASIS_PARTS + CELLS // PART + 1,)),
+        ],
+        compiler_params=pltpu.CompilerParams(vmem_limit_bytes=32 * 2**20),
+    )(*held)
 
 
 def per_device(snapshots, conductivity, storage):

time: 38.7 us -> 34.9 us (0.902)
  Pallas kernels: 37.9 us -> 34.1 us
    pallas_call x1, Pallas kernels: 34 us -> 30.5 us  [gathered(): pl.pallas_call(gather_kernel, out_shape=(pltpu.VMEM((K * PITCH, TY), F32)...]
where the time goes in v3:
time: 34.9 us; the launch traced here: 34.8 us
  Pallas kernels  34.1 us (98%)
  between operations  0.64 us (2%)
    pallas_call x1, Pallas kernels, gathered(): pl.pallas_call(gather_kernel, out_shape=(pltpu.VMEM((K * PITCH, TY), F32)...  30.5 us
    pallas_call x1, Pallas kernels, written(): pl.pallas_call(write_kernel, out_shape=(shape, shape, jax.ShapeDtypeStruc...  3.66 us

profile of v3, /device:TPU:1, one launch (start us, length us, event | category | flops | bytes accessed | tf_op | source)
XLA Modules:
  0.0 34.8 jit_solution(6288133717299130065)
XLA Ops:
  0.6 30.5 %shard_map.58 = (f32[8704,128]{1,0:T(8,128)S(1)}, bf16[128,128,128]{2,1,0:T(8,128)(2,1)S(1)}, bf16[64,256]{1,0:T(8,128)(2,1)S(1)}, f32[2,64,128]{2,1,0:T(8,128)S...) custom-call(f32[64,128,128]{2,1,0:T(8,128)} %bitcast.5, f32[128,128]{1,0:T(8,128)} %bitcast.6, f32[128,128]{1,0:T(8,128)} %bitcast.7), custom_call_target="tpu_custom_call" | custom-call | tf_op jit(solution)/shard_map/pallas_call | solution.py:437
  31.1 3.7 %shard_map.59 = (f32[64,128,128]{2,1,0:T(8,128)}, f32[64,128,128]{2,1,0:T(8,128)}, f32[64,64]{1,0:T(8,128)}) custom-call(f32[8704,128]{1,0:T(8,128)S(1)} %get-tuple-element.12.basis_held, bf16[128,128,128]{2,1,0:T(8,128)(2,1)S(1)} %get-tuple-element.13.flux, bf16[64,256]{1,0:T(8,128)(2,1)S(1)} %get-tuple-element.14.wide, ...), custom_call_target="tpu_custom_call" | custom-call | tf_op jit(solution)/shard_map/pallas_call | solution.py:532

commit v4 on v3

--- a/solution.py
+++ b/solution.py
@@ -39,16 +39,37 @@
     return lax.broadcasted_iota(jnp.int32, shape, len(shape) - 2)
 
 
+SHARE = 9
+HALF = K // 2
+
+
 def folded(matrix):
+    def laid(block, last):
+        quarters = [block[8 * i : 8 * i + 8] for i in range(4)]
+        return jnp.concatenate([jnp.concatenate(quarters, axis=1), last], axis=0)
+
+    row, column = rows((HALF, HALF)), lanes((HALF, HALF))
+    first, second = matrix[:HALF, :HALF], matrix[HALF:, HALF:]
+    diagonal = jnp.sum(jnp.where(row == column, second, 0.0), axis=0, keepdims=True)
+    none = jnp.zeros((1, 128 - HALF), F32)
     return [
-        jnp.concatenate([matrix[32 * h : 32 * h + 16], matrix[32 * h + 16 : 32 * h + 32]], axis=1)
-        for h in range(2)
+        laid(matrix[:HALF, HALF:], jnp.zeros((1, 128), F32)),
+        laid(jnp.where(column >= row, first, second), jnp.concatenate([diagonal, none], axis=1)),
     ]
 
 
-def unfolded(halves):
+def unfolded(shares):
+    def block(share):
+        return jnp.concatenate([share[0:8, HALF * i : HALF * i + HALF] for i in range(4)], axis=0)
+
+    row, column = rows((HALF, HALF)), lanes((HALF, HALF))
+    corner, both = block(shares[0]), block(shares[1])
+    upper = jnp.where(column > row, both, 0.0)
+    lower = jnp.where(column < row, both, 0.0)
+    first = jnp.where(column >= row, both, 0.0) + upper.T
+    second = lower + lower.T + jnp.where(column == row, shares[1][8:9, :HALF], 0.0)
     return jnp.concatenate(
-        [part for h in halves for part in (h[:, :64], h[:, 64:])], axis=0
+        [jnp.concatenate([first, corner], axis=1), jnp.concatenate([corner.T, second], axis=1)], axis=0
     )
 
 
@@ -160,47 +181,32 @@
     return whole[:, K:] * (1.0 / jnp.sqrt(pivots))
 
 
-UNROLL0 = 8
-UNROLL1 = 8
-UNROLL2 = 5
-UNROLL3 = 32
-
-
-def edge_pass(l, natural, field, edges):
+def first_pass(first, natural, field, snap, edges, gram_acc):
     lane = lanes((K, TY))
 
-    def four_rows(turn, carry):
-        kept = [edges[0], edges[1]]
-        for d in range(4):
-            x = turn * 4 + d
-            cell = l * TX + x
-            value = natural[pl.ds(cell, K, stride=PITCH), :]
-            field[x + 1, l] = value
-            turned = pltpu.roll(value, cell, 1)
-            here = (lane == cell) | (lane == lax.rem(cell + TY - 1, TY))
-            kept[d % 2] = jnp.where(here, turned, kept[d % 2])
-        edges[0], edges[1] = kept
-        return carry
-
-    lax.fori_loop(0, TX // 4, four_rows, 0, unroll=UNROLL0)
-
-
-def gram_pass(field, snap, gram_acc):
-    def one_row(x, carry):
+    def two_rows(turn, carry):
         highs, lows = [], []
-        for l in range(LAYERS):
-            cell = l * TX + x
-            high, low = split(field[x + 1, l])
-            snap[cell, 0:K] = high
-            snap[cell, K : 2 * K] = low
-            highs.append(high)
-            lows.append(low)
+        for d in range(2):
+            x = first + turn * 2 + d
+            kept = edges[d]
+            for l in range(LAYERS):
+                cell = l * TX + x
+                value = natural[pl.ds(cell, K, stride=PITCH), :]
+                field[x + 1, l] = value
+                here = (lane == cell) | (lane == lax.rem(cell + TY - 1, TY))
+                kept = jnp.where(here, pltpu.roll(value, cell, 1), kept)
+                high, low = split(value)
+                snap[cell, 0:K] = high
+                snap[cell, K : 2 * K] = low
+                highs.append(high)
+                lows.append(low)
+            edges[d] = kept
         high = jnp.concatenate(highs, axis=1)
         low = jnp.concatenate(lows, axis=1)
         gram_acc[...] += product_nt(jnp.concatenate([high, low], axis=0), high)
         return carry
 
-    lax.fori_loop(0, TX, one_row, 0, unroll=UNROLL1)
+    lax.fori_loop(0, 4, two_rows, 0, unroll=True)
 
 
 def expand_pass(weights, source, held):
@@ -212,7 +218,7 @@
         held[pl.ds(cell + 1, K, stride=PITCH), :] = out[:, TY:]
         return carry
 
-    lax.fori_loop(0, CELLS // 2, two_cells, 0, unroll=UNROLL3)
+    lax.fori_loop(0, CELLS // 2, two_cells, 0, unroll=True)
 
 
 def local_coefficients(cond, stor, coefs):
@@ -271,12 +277,12 @@
     )
 
 
-def second_pass(coefs, field, snap, flux, proj_acc):
+def second_pass(first, last, coefs, field, snap, flux, proj_acc):
     def two_rows(turn, carry):
         flux_rows((1 + 2 * turn, 2 + 2 * turn), coefs, field, snap, flux, proj_acc)
         return carry
 
-    lax.fori_loop(0, TX // 2 - 1, two_rows, 0, unroll=UNROLL2)
+    lax.fori_loop(first, last, two_rows, 0, unroll=True)
 
 
 def gather_kernel(
@@ -296,12 +302,16 @@
 
     natural3 = natural.reshape(K, PITCH, TY)
     loads = [
-        pltpu.make_async_copy(cond_any, cond, load_sem.at[LAYERS]),
-        pltpu.make_async_copy(stor_any, stor, load_sem.at[LAYERS + 1]),
+        pltpu.make_async_copy(cond_any, cond, load_sem.at[16]),
+        pltpu.make_async_copy(stor_any, stor, load_sem.at[17]),
     ]
-    for l in range(LAYERS):
-        part = pl.ds(l * TX, TX)
-        loads.append(pltpu.make_async_copy(snap_any.at[:, part], natural3.at[:, part], load_sem.at[l]))
+    order = (0, 3, 1, 2)
+    for b in order:
+        for l in range(LAYERS):
+            part = pl.ds(l * TX + 8 * b, 8)
+            loads.append(
+                pltpu.make_async_copy(snap_any.at[:, part], natural3.at[:, part], load_sem.at[l * 4 + b])
+            )
     for load in loads:
         load.start()
 
@@ -329,14 +339,6 @@
     end_send[0, K : K + 8] = turned[0:8]
     end_send[1, K : K + 8] = turned[TY - 8 : TY]
 
-    for l in range(LAYERS):
-        loads[2 + l].wait()
-        edge_pass(l, natural, field, edges)
-
-    even = lax.rem(lanes((K, TY)), 2) == 0
-    end_send[0, 0:K] = jnp.where(even, edges[0], edges[1])
-    end_send[1, 0:K] = pltpu.roll(jnp.where(even, edges[1], edges[0]), 1, 1)
-
     def halo(src, dst, which, device):
         copy = pltpu.make_async_remote_copy(
             src_ref=src, dst_ref=dst, send_sem=halo_send.at[which], recv_sem=halo_recv.at[which],
@@ -345,24 +347,33 @@
         copy.start()
         return copy
 
-    pl.semaphore_wait(barrier, len(partners))
-    x_halos = [
-        halo(field.at[1], field.at[TX + 1], 0, x_left),
-        halo(field.at[TX], field.at[0], 1, x_right),
-        halo(side_send.at[0], side_got.at[1], 2, x_left),
-        halo(side_send.at[1], side_got.at[0], 3, x_right),
-    ]
+    for at, b in enumerate(order):
+        if at == 3:
+            pl.semaphore_wait(barrier, len(partners))
+            x_halos = [
+                halo(field.at[1], field.at[TX + 1], 0, x_left),
+                halo(field.at[TX], field.at[0], 1, x_right),
+                halo(side_send.at[0], side_got.at[1], 2, x_left),
+                halo(side_send.at[1], side_got.at[0], 3, x_right),
+            ]
+        for l in range(LAYERS):
+            loads[2 + at * LAYERS + l].wait()
+        first_pass(8 * b, natural, field, snap, edges, gram_acc)
+
+    cross = gram_acc[K : 2 * K]
+    gram_total.start_pair(gram_acc[0:K] + (cross + cross.T))
+
+    even = lax.rem(lanes((K, TY)), 2) == 0
+    end_send[0, 0:K] = jnp.where(even, edges[0], edges[1])
+    end_send[1, 0:K] = pltpu.roll(jnp.where(even, edges[1], edges[0]), 1, 1)
+
     y_halos = [
         halo(end_send.at[0], end_got.at[1], 4, y_left),
         halo(end_send.at[1], end_got.at[0], 5, y_right),
     ]
-
-    gram_pass(field, snap, gram_acc)
-    cross = gram_acc[K : 2 * K]
-    gram_total.start_pair(gram_acc[0:K] + (cross + cross.T))
+    second_pass(0, 5, coefs, field, snap, flux, proj_acc)
     gram_total.start_plane()
-
-    second_pass(coefs, field, snap, flux, proj_acc)
+    second_pass(5, TX // 2 - 1, coefs, field, snap, flux, proj_acc)
 
     for copy in x_halos:
         copy.wait_recv()
@@ -403,8 +414,8 @@
     proj_total.start_pair(proj_part)
     proj_total.start_plane()
     gram_total.start_column()
+    proj_total.start_column()
     gram_total.start_whole()
-    proj_total.start_column()
     weights = eliminated(gram_total.result() * (1.0 / COUNT))
     weights_out[...] = weights
     high, low = split(weights)
@@ -427,11 +438,11 @@
     any_spec = pl.BlockSpec(memory_space=pltpu.HBM)
     vmem_spec = pl.BlockSpec(memory_space=pltpu.VMEM)
     total = [
-        pltpu.VMEM((2, 16, 128), F32),
-        pltpu.VMEM((16, 128), F32),
-        pltpu.VMEM((XY, 16, 128), F32),
-        pltpu.VMEM((Z, 16, 128), F32),
-        pltpu.VMEM((2, 16, 128), F32),
+        pltpu.VMEM((2, SHARE, 128), F32),
+        pltpu.VMEM((SHARE, 128), F32),
+        pltpu.VMEM((XY, SHARE, 128), F32),
+        pltpu.VMEM((Z, SHARE, 128), F32),
+        pltpu.VMEM((2, SHARE, 128), F32),
     ]
     dma = pltpu.SemaphoreType.DMA
     return pl.pallas_call(
@@ -462,7 +473,7 @@
             pltpu.VMEM((2, K + 8, TY), F32),
             *total,
             *total,
-            dma((LAYERS + 2,)),
+            dma((18,)),
             dma((6,)),
             dma((6,)),
             dma((4,)),

time: 34.9 us -> 33.7 us (0.966)
  Pallas kernels: 34.1 us -> 32.9 us
    pallas_call x1, Pallas kernels: 30.5 us -> 29.3 us  [gathered(): pl.pallas_call(gather_kernel, out_shape=(pltpu.VMEM((K * PITCH, TY), F32)...]
where the time goes in v4:
time: 33.7 us; the launch traced here: 33.6 us
  Pallas kernels  32.9 us (98%)
  between operations  0.64 us (2%)
    pallas_call x1, Pallas kernels, gathered(): pl.pallas_call(gather_kernel, out_shape=(pltpu.VMEM((K * PITCH, TY), F32)...  29.3 us
    pallas_call x1, Pallas kernels, written(): pl.pallas_call(write_kernel, out_shape=(shape, shape, jax.ShapeDtypeStruc...  3.66 us

profile of v4, /device:TPU:1, one launch (start us, length us, event | category | flops | bytes accessed | tf_op | source)
XLA Modules:
  0.0 33.6 jit_solution(974440366914005357)
XLA Ops:
  0.6 29.3 %shard_map.58 = (f32[8704,128]{1,0:T(8,128)S(1)}, bf16[128,128,128]{2,1,0:T(8,128)(2,1)S(1)}, bf16[64,256]{1,0:T(8,128)(2,1)S(1)}, f32[2,64,128]{2,1,0:T(8,128)S...) custom-call(f32[64,128,128]{2,1,0:T(8,128)} %bitcast.5, f32[128,128]{1,0:T(8,128)} %bitcast.6, f32[128,128]{1,0:T(8,128)} %bitcast.7), custom_call_target="tpu_custom_call" | custom-call | tf_op jit(solution)/shard_map/pallas_call | solution.py:448
  29.9 3.7 %shard_map.59 = (f32[64,128,128]{2,1,0:T(8,128)}, f32[64,128,128]{2,1,0:T(8,128)}, f32[64,64]{1,0:T(8,128)}) custom-call(f32[8704,128]{1,0:T(8,128)S(1)} %get-tuple-element.12.basis_held, bf16[128,128,128]{2,1,0:T(8,128)(2,1)S(1)} %get-tuple-element.13.flux, bf16[64,256]{1,0:T(8,128)(2,1)S(1)} %get-tuple-element.14.wide, ...), custom_call_target="tpu_custom_call" | custom-call | tf_op jit(solution)/shard_map/pallas_call | solution.py:543

commit v5 on v4

--- a/solution.py
+++ b/solution.py
@@ -74,9 +74,9 @@
 
 
 class Total:
-    def __init__(self, place, packed, pair, plane, column, whole, send, recv):
+    def __init__(self, place, packed, plane, column, send, recv):
         self.x, self.y, self.z, self.core = place
-        self.packed, self.pair, self.plane, self.column, self.whole = packed, pair, plane, column, whole
+        self.packed, self.plane, self.column = packed, plane, column
         self.send, self.recv = send, recv
 
     def device(self, x, y, z, core):
@@ -92,64 +92,56 @@
             device_id_type=MESH,
         ).start()
 
-    def other_core(self):
-        return self.device(self.x, self.y, self.z, 1 - self.core)
-
     def plane_peers(self):
+        cores = (self.core, 1 - self.core)
         return [
-            self.device(lax.rem(self.x + i, 4), lax.rem(self.y + j, 4), self.z, self.core)
+            (core, self.device(lax.rem(self.x + i, 4), lax.rem(self.y + j, 4), self.z, core))
             for i in range(4)
             for j in range(4)
-            if i or j
+            for at, core in enumerate(cores)
+            if i or j or at
         ]
 
     def column_peers(self):
-        return [self.device(self.x, self.y, lax.rem(self.z + i, Z), self.core) for i in range(1, Z)]
-
-    def start_pair(self, matrix):
-        for h, half in enumerate(folded(matrix)):
-            self.packed[h] = half
-        self.copy(self.packed.at[1 - self.core], self.pair, 0, self.other_core())
-
-    def start_plane(self):
-        pltpu.make_async_copy(self.pair, self.pair, self.recv.at[0]).wait()
-        me = self.x * 4 + self.y
-        self.plane[me] = self.packed[self.core] + self.pair[...]
-        for peer in self.plane_peers():
-            self.copy(self.plane.at[me], self.plane.at[me], 1, peer)
+        return [
+            self.device(self.x, self.y, lax.rem(self.z + i, Z), core)
+            for i in range(Z)
+            for at, core in enumerate((self.core, 1 - self.core))
+            if i or at
+        ]
+
+    def start_plane(self, matrix):
+        for core, share in enumerate(folded(matrix)):
+            self.packed[core] = share
+        me = (self.x * 4 + self.y) * 2 + self.core
+        for core, peer in self.plane_peers():
+            self.copy(self.packed.at[core], self.plane.at[me], 0, peer)
+        self.plane[me] = self.packed[self.core]
 
     def start_column(self):
-        rest = self.plane.at[pl.ds(0, XY - 1)]
+        rest = self.plane.at[pl.ds(0, 2 * XY - 1)]
+        pltpu.make_async_copy(rest, rest, self.recv.at[0]).wait()
+        total = self.plane[0]
+        for i in range(1, 2 * XY):
+            total = total + self.plane[i]
+        me = self.core * Z + self.z
+        self.column[me] = total
+        for peer in self.column_peers():
+            self.copy(self.column.at[me], self.column.at[me], 1, peer)
+
+    def result(self):
+        rest = self.column.at[pl.ds(0, 2 * Z - 1)]
         pltpu.make_async_copy(rest, rest, self.recv.at[1]).wait()
-        total = self.plane[0]
-        for i in range(1, XY):
-            total = total + self.plane[i]
-        self.column[self.z] = total
-        for peer in self.column_peers():
-            self.copy(self.column.at[self.z], self.column.at[self.z], 2, peer)
-
-    def start_whole(self):
-        rest = self.column.at[pl.ds(0, Z - 1)]
-        pltpu.make_async_copy(rest, rest, self.recv.at[2]).wait()
-        total = self.column[0]
-        for i in range(1, Z):
-            total = total + self.column[i]
-        self.whole[self.core] = total
-        self.copy(self.whole.at[self.core], self.whole.at[self.core], 3, self.other_core())
-
-    def result(self):
-        pltpu.make_async_copy(self.whole.at[0], self.whole.at[0], self.recv.at[3]).wait()
-        return unfolded([self.whole[0], self.whole[1]])
+        shares = []
+        for core in range(2):
+            total = self.column[core * Z]
+            for i in range(1, Z):
+                total = total + self.column[core * Z + i]
+            shares.append(total)
+        return unfolded(shares)
 
     def drain(self):
-        for step, ref in enumerate(
-            (
-                self.pair,
-                self.plane.at[pl.ds(0, XY - 1)],
-                self.column.at[pl.ds(0, Z - 1)],
-                self.whole.at[0],
-            )
-        ):
+        for step, ref in enumerate((self.plane.at[pl.ds(0, 2 * XY - 1)], self.column.at[pl.ds(0, 2 * Z - 1)])):
             pltpu.make_async_copy(ref, ref, self.send.at[step]).wait()
 
 
@@ -291,14 +283,14 @@
     snap, natural, field, cond, stor, coefs, edges,
     gram_acc, proj_acc,
     side_send, side_got, end_send, end_got,
-    g_packed, g_pair, g_plane, g_column, g_whole,
-    m_packed, m_pair, m_plane, m_column, m_whole,
+    g_packed, g_plane, g_column,
+    m_packed, m_plane, m_column,
     load_sem, halo_send, halo_recv, g_send, g_recv, m_send, m_recv,
 ):
     gx, gy = lax.axis_index("gx"), lax.axis_index("gy")
     place = (gx // 2, lax.rem(gy, 4), gy // 4, lax.rem(gx, 2))
-    gram_total = Total(place, g_packed, g_pair, g_plane, g_column, g_whole, g_send, g_recv)
-    proj_total = Total(place, m_packed, m_pair, m_plane, m_column, m_whole, m_send, m_recv)
+    gram_total = Total(place, g_packed, g_plane, g_column, g_send, g_recv)
+    proj_total = Total(place, m_packed, m_plane, m_column, m_send, m_recv)
 
     natural3 = natural.reshape(K, PITCH, TY)
     loads = [
@@ -320,7 +312,7 @@
     y_left = (gx, lax.rem(gy + 31, 32))
     y_right = (gx, lax.rem(gy + 1, 32))
     barrier = pltpu.get_barrier_semaphore()
-    partners = [gram_total.other_core(), *gram_total.plane_peers(), *gram_total.column_peers()]
+    partners = [peer for _, peer in gram_total.plane_peers()] + gram_total.column_peers()
     partners += [x_left, x_right, y_left, y_right]
     for partner in partners:
         pl.semaphore_signal(barrier, inc=1, device_id=partner, device_id_type=MESH)
@@ -361,7 +353,7 @@
         first_pass(8 * b, natural, field, snap, edges, gram_acc)
 
     cross = gram_acc[K : 2 * K]
-    gram_total.start_pair(gram_acc[0:K] + (cross + cross.T))
+    gram_total.start_plane(gram_acc[0:K] + (cross + cross.T))
 
     even = lax.rem(lanes((K, TY)), 2) == 0
     end_send[0, 0:K] = jnp.where(even, edges[0], edges[1])
@@ -371,9 +363,7 @@
         halo(end_send.at[0], end_got.at[1], 4, y_left),
         halo(end_send.at[1], end_got.at[0], 5, y_right),
     ]
-    second_pass(0, 5, coefs, field, snap, flux, proj_acc)
-    gram_total.start_plane()
-    second_pass(5, TX // 2 - 1, coefs, field, snap, flux, proj_acc)
+    second_pass(0, TX // 2 - 1, coefs, field, snap, flux, proj_acc)
 
     for copy in x_halos:
         copy.wait_recv()
@@ -411,11 +401,9 @@
     proj_part = lax.dot_general(ends, rim, (((1,), (1,)), ((), ())), **exact) + (
         proj_acc[0:K, 0:K] + (proj_acc[K : 2 * K, 0:K] + proj_acc[0:K, K : 2 * K]) + proj_acc[K : 2 * K, K : 2 * K]
     )
-    proj_total.start_pair(proj_part)
-    proj_total.start_plane()
+    proj_total.start_plane(proj_part)
     gram_total.start_column()
     proj_total.start_column()
-    gram_total.start_whole()
     weights = eliminated(gram_total.result() * (1.0 / COUNT))
     weights_out[...] = weights
     high, low = split(weights)
@@ -425,7 +413,6 @@
     left, right = rim[:, :TY], pltpu.roll(rim[:, TY:], TY - 1, 1)
     rim_out[0] = jnp.where(even, left, right)
     rim_out[1] = jnp.where(even, right, left)
-    proj_total.start_whole()
     expand_pass(wide, snap, basis_held)
     proj_out[...] = proj_total.result()
     for copy in x_halos + y_halos:
@@ -439,10 +426,8 @@
     vmem_spec = pl.BlockSpec(memory_space=pltpu.VMEM)
     total = [
         pltpu.VMEM((2, SHARE, 128), F32),
-        pltpu.VMEM((SHARE, 128), F32),
-        pltpu.VMEM((XY, SHARE, 128), F32),
-        pltpu.VMEM((Z, SHARE, 128), F32),
-        pltpu.VMEM((2, SHARE, 128), F32),
+        pltpu.VMEM((2 * XY, SHARE, 128), F32),
+        pltpu.VMEM((2 * Z, SHARE, 128), F32),
     ]
     dma = pltpu.SemaphoreType.DMA
     return pl.pallas_call(
@@ -476,10 +461,10 @@
             dma((18,)),
             dma((6,)),
             dma((6,)),
-            dma((4,)),
-            dma((4,)),
-            dma((4,)),
-            dma((4,)),
+            dma((2,)),
+            dma((2,)),
+            dma((2,)),
+            dma((2,)),
         ],
         compiler_params=pltpu.CompilerParams(
             collective_id=0, has_side_effects=True, vmem_limit_bytes=40 * 2**20

time: 33.7 us -> 32.4 us (0.961)
  Pallas kernels: 32.9 us -> 31.7 us
    pallas_call x1, Pallas kernels: 29.3 us -> 28 us  [gathered(): pl.pallas_call(gather_kernel, out_shape=(pltpu.VMEM((K * PITCH, TY), F32)...]
where the time goes in v5:
time: 32.4 us; the launch traced here: 32.3 us
  Pallas kernels  31.7 us (98%)
  between operations  0.64 us (2%)
    pallas_call x1, Pallas kernels, gathered(): pl.pallas_call(gather_kernel, out_shape=(pltpu.VMEM((K * PITCH, TY), F32)...  28 us
    pallas_call x1, Pallas kernels, written(): pl.pallas_call(write_kernel, out_shape=(shape, shape, jax.ShapeDtypeStruc...  3.66 us

profile of v5, /device:TPU:1, one launch (start us, length us, event | category | flops | bytes accessed | tf_op | source)
XLA Modules:
  0.0 32.3 jit_solution(6334929927148381131)
XLA Ops:
  0.6 28.0 %shard_map.58 = (f32[8704,128]{1,0:T(8,128)S(1)}, bf16[128,128,128]{2,1,0:T(8,128)(2,1)S(1)}, bf16[64,256]{1,0:T(8,128)(2,1)S(1)}, f32[2,64,128]{2,1,0:T(8,128)S...) custom-call(f32[64,128,128]{2,1,0:T(8,128)} %bitcast.5, f32[128,128]{1,0:T(8,128)} %bitcast.6, f32[128,128]{1,0:T(8,128)} %bitcast.7), custom_call_target="tpu_custom_call" | custom-call | tf_op jit(solution)/shard_map/pallas_call | solution.py:433
  28.6 3.7 %shard_map.59 = (f32[64,128,128]{2,1,0:T(8,128)}, f32[64,128,128]{2,1,0:T(8,128)}, f32[64,64]{1,0:T(8,128)}) custom-call(f32[8704,128]{1,0:T(8,128)S(1)} %get-tuple-element.12.basis_held, bf16[128,128,128]{2,1,0:T(8,128)(2,1)S(1)} %get-tuple-element.13.flux, bf16[64,256]{1,0:T(8,128)(2,1)S(1)} %get-tuple-element.14.wide, ...), custom_call_target="tpu_custom_call" | custom-call | tf_op jit(solution)/shard_map/pallas_call | solution.py:528
